TPU v7x, 128 devices: a whole 4x4x4 slice. The times are simulated.
128 devices in a mesh: mc: 8 (over z, core), space: 16 (over x, y).
Axes of the slice: x: 4, y: 4, z: 4, core: 2. Of those that a mesh axis runs over, the one named last changes fastest.
Arguments:
- orbit_state: float32 [6, 4194304], P(None, ('mc', 'space')), parts along dimension 1, may hold values from -1.3 to 1.3, as said below
- object_props: float32 [3, 4194304], P(None, ('mc', 'space')), parts along dimension 1, may hold values from 0.5 to 2
- density_table: float32 [64], replicated, may hold values from -1 to 1
- block_cube: int32 [32768], P(('mc', 'space')), parts along dimension 0, may hold values from 0 to 2047, as said below
Outputs:
- next_state: float32 [6, 4194304], P(None, ('mc', 'space')), parts along dimension 1
- collision_rate: float32 [4194304], P(('mc', 'space')), parts along dimension 0
There are 8 independent parts, one for each index of `mc`. A program takes and returns all parts, laid end to end along the dimension named above; an argument that names none is the same for every part. Nothing has to cross between parts.
Inputs may be any that keep to these rules, and one draw needn't show every extreme that they name: `orbit_state`: rows 0 to 2 are a position with 1.08 <= |r| <= 1.3, rows 3 to 5 a velocity of speed between 0.86 and 0.98. `block_cube`: cube c is owned by the device of index c // 128 along space. No cube holds more than 4 blocks in all, and in every draw some cube holds exactly 4. The blocks of one device include at most 32 whose cubes have any one owner, and in every draw some owner receives exactly 32 blocks from every device.
All inputs are finite; a program needn't handle non-finite values.
Results may differ from a plain program's by a relative error of at most 0.0003.
Values sent between devices are 32-bit elements; how exact they have to be, the bound alone decides.
A program may use at most 64 MiB of HBM per device.

v0:
```python
import math

import jax
import jax.numpy as jnp
from jax import lax
from jax.sharding import PartitionSpec as P

BLK = 128
MOST = 4
SUB = 16
NTAB = 64


TIME_STEP = 0.2
EARTH_SPIN = 0.0588
J2_COEF = 0.00108263
DRAG_SCALE = 0.008
SCALE_HEIGHT = 0.1
TABLE_TOP = 0.4
SPEED_FLOOR = 0.04


def propagate(orbit_part, prop_part, density_table):
    position = orbit_part[0:3]
    velocity = orbit_part[3:6]
    ballistic = prop_part[2]
    alt_grid = jnp.arange(NTAB).astype(density_table.dtype)
    for substep in range(SUB):
        radius_sq = jnp.sum(position * position, axis=0)
        radius = jnp.sqrt(radius_sq)
        height = radius - 1.0
        table_coord = height * ((NTAB - 1) / TABLE_TOP)
        hat_weights = jnp.maximum(0.0, 1.0 - jnp.abs(table_coord[None, :] - alt_grid[:, None]))
        log_density = (
            jnp.dot(density_table[None, :], hat_weights, precision=lax.Precision.HIGHEST)[0]
            - height / SCALE_HEIGHT
        )
        density = DRAG_SCALE * jnp.exp(log_density)
        relative = jnp.stack(
            [
                velocity[0] + EARTH_SPIN * position[1],
                velocity[1] - EARTH_SPIN * position[0],
                velocity[2],
            ]
        )
        air_speed = jnp.sqrt(jnp.sum(relative * relative, axis=0))
        inv_cube = 1.0 / (radius_sq * radius)
        polar_ratio = position[2] * position[2] / radius_sq
        oblate_factor = 1.5 * J2_COEF / (radius_sq * radius_sq * radius)
        shape_term = jnp.stack(
            [1.0 - 5.0 * polar_ratio, 1.0 - 5.0 * polar_ratio, 3.0 - 5.0 * polar_ratio]
        )
        acceleration = (
            -position * inv_cube
            - oblate_factor * position * shape_term
            - density * ballistic * air_speed * relative
        )
        velocity = velocity + TIME_STEP * acceleration
        position = position + TIME_STEP * velocity
    return jnp.concatenate([position, velocity], axis=0)


def propagate_all(orbit_state, object_props, density_table):
    total_count = orbit_state.shape[1]
    span_width = math.gcd(total_count, 4096)
    groups = total_count // span_width
    stacked = orbit_state.reshape(6, groups, span_width).transpose(1, 0, 2)
    prop_stack = object_props.reshape(3, groups, span_width).transpose(1, 0, 2)
    advanced = lax.map(
        lambda packed: propagate(packed[0], packed[1], density_table), (stacked, prop_stack)
    )
    return advanced.transpose(1, 0, 2).reshape(6, total_count)


def tile_rates(own_rows, mate_rows, column_ok, self_column):
    group_size = own_rows.shape[1]
    span_width = mate_rows.shape[2]
    diff_sq = jnp.zeros((group_size, BLK, span_width), own_rows.dtype)
    for component in range(3):
        velocity_gap = own_rows[component][:, :, None] - mate_rows[component][:, None, :]
        diff_sq = diff_sq + velocity_gap * velocity_gap
    same_index = (jnp.arange(BLK)[:, None] == (jnp.arange(span_width) % BLK)[None, :])[None, :, :]
    keep_mask = column_ok[:, None, :] & jnp.logical_not(self_column[:, None, :] & same_index)
    pair_term = jnp.where(
        keep_mask,
        mate_rows[4][:, None, :]
        * (own_rows[3][:, :, None] + mate_rows[3][:, None, :]) ** 2
        * jnp.sqrt(diff_sq + SPEED_FLOOR),
        0.0,
    )
    return own_rows[4] * jnp.sum(pair_term, axis=2) / span_width


def find_partners(cube_value):
    slot_count = cube_value.shape[0]
    slot_index = jnp.arange(slot_count)
    live_slot = cube_value >= 0.0
    same_cube = (cube_value[:, None] == cube_value[None, :]) & live_slot[:, None]
    scores = jnp.where(
        same_cube, 2 * slot_count - slot_index[None, :], slot_count - slot_index[None, :]
    )
    values, partners = lax.top_k(scores, MOST)
    return (partners, values > slot_count)


def owner_groups(received, partners, partner_ok):
    slot_count = received.shape[1]
    group_size = math.gcd(slot_count, 32)

    def one_group(first_block):
        group_ids = first_block + jnp.arange(group_size)
        group_mates = jnp.take(partners, group_ids, axis=0)
        own_rows = jnp.take(received, group_ids, axis=1)
        mate_rows = jnp.take(received, group_mates.reshape(group_size * MOST), axis=1).reshape(
            5, group_size, MOST * BLK
        )
        column_ok = jnp.repeat(jnp.take(partner_ok, group_ids, axis=0), BLK, axis=1)
        self_column = jnp.repeat(group_mates == group_ids[:, None], BLK, axis=1)
        return tile_rates(own_rows, mate_rows, column_ok, self_column)

    block_rates = lax.map(one_group, jnp.arange(0, slot_count, group_size))
    return block_rates.reshape(slot_count, BLK)


def on_device(orbit_state, object_props, density_table, block_cube):
    space_size = lax.axis_size("space")
    block_count = block_cube.shape[0]
    object_count = orbit_state.shape[1]
    next_state = propagate_all(orbit_state, object_props, density_table)
    capacity = (2 * block_count + space_size - 1) // space_size
    slot_count = space_size * capacity
    cubes_owned = slot_count // MOST
    block_owner = block_cube // cubes_owned
    onehot = (block_owner[:, None] == jnp.arange(space_size)[None, :]).astype(jnp.int32)
    slot_rank = jnp.sum((jnp.cumsum(onehot, axis=0) - onehot) * onehot, axis=1)
    block_slot = block_owner * capacity + slot_rank
    matches = block_slot[None, :] == jnp.arange(slot_count)[:, None]
    filled = jnp.any(matches, axis=1)
    source = jnp.sum(jnp.where(matches, jnp.arange(block_count)[None, :], 0), axis=1)
    cube_out = jnp.where(filled, jnp.take(block_cube, source), -1).astype(jnp.float32)[None, :]
    records = jnp.concatenate([next_state[3:6], object_props[0:2]], axis=0)
    own_all = records.reshape(5, block_count, BLK)
    outgoing = jnp.where(filled[None, :, None], jnp.take(own_all, source, axis=1), 0.0)
    received, cube_in = (
        lax.all_to_all(outgoing, "space", split_axis=1, concat_axis=1, tiled=True),
        lax.all_to_all(cube_out, "space", split_axis=1, concat_axis=1, tiled=True),
    )
    partners, partner_ok = find_partners(cube_in[0])
    block_rates = owner_groups(received, partners, partner_ok)
    returned = lax.all_to_all(block_rates, "space", split_axis=0, concat_axis=0, tiled=True)
    own_rates = jnp.take(returned, block_slot, axis=0).reshape(object_count)
    return (next_state, own_rates)


def solution(mesh):
    placed = (P(None, ("mc", "space")), P(None, ("mc", "space")), P(), P(("mc", "space")))
    return jax.shard_map(
        on_device,
        mesh=mesh,
        in_specs=placed,
        out_specs=(P(None, ("mc", "space")), P(("mc", "space"))),
        check_vma=False,
    )
```

profile of v0, /device:TPU:0, one launch (start us, length us, event | category | flops | bytes accessed | tf_op | source)
XLA Modules:
  0.0 599.3 jit_solution(15517749754106236483)
XLA Ops:
  10.6 3.6 gather_fusion.5
  15.0 7.1 %all-to-all-start.1 = ((f32[1,16,32]{2,0,1:T(1,128)}), f32[1,16,32]{2,0,1:T(1,128)S(1)}, u32[]{:S(2)}, u32[]{:S(2)}) async-start(f32[1,16,32]{2,0,1:T(1,128)} %bitcast.79), calls=%async_computation.1 | async-start | bytes 16384 | tf_op jit(solution)/shard_map/all_to_all | solution.py:146
  22.4 200.7 %while.25 = (s32[]{:T(128)}, f32[8,6,4096]{2,1,0:T(8,128)S(1)}, f32[8,6,4096]{2,1,0:T(8,128)}, f32[64]{0:T(128)S(1)}, f32[8,3,4096]{2,1,0:T(4,128)S(1)}, /*index...) while((s32[]{:T(128)}, f32[8,6,4096]{2,1,0:T(8,128)S(1)}, f32[8,6,4096]{2,1,0:T(8,128)}, ...), condition=%wide.region_33.34_spmd, body=%wide.region_0.33_spmd.sunk | while | flops 72573000 | bytes 13459941 | solution.py:69
  22.4 1.5 fusion.535
  47.6 1.3 fusion.535
  72.6 1.3 fusion.535
  97.6 1.3 fusion.535
  122.6 1.3 fusion.535
  147.7 1.4 fusion.535
  224.0 1.9 gather_fusion.4
  229.6 3.4 select_bitcast_fusion.2
  233.0 7.2 %all-to-all-start = ((f32[5,512,128]{2,0,1:T(8,128)}), f32[5,512,128]{2,0,1:T(8,128)S(1)}, u32[]{:S(2)}, u32[]{:S(2)}) async-start(f32[5,512,128]{2,0,1:T(8,128)} %select_bitcast_fusion.2), calls=%async_computation | async-start | bytes 4194304 | tf_op jit(solution)/shard_map/all_to_all | solution.py:145
  240.2 34.5 %top_k.23.cloned.1.call-done = (s32[512,512]{1,0:T(8,128)}, s32[512,512]{1,0:T(8,128)}) async-done(((s32[512,512]{1,0:T(8,128)}, s32[512,512]{1,0:T(8,128)}), (s32[512,512]{1,0:T(8,128)}, s32[512,512]{1,0:T(8,128)})) %top_k.23.cloned.1.call-update) | async-done | bytes 2097168 | tf_op jit(solution)/shard_map/top_k | solution.py:102
  276.7 298.1 %while.26 = (s32[]{:T(128)}, f32[16,32,128]{2,1,0:T(8,128)}, s32[16]{0:T(128)S(1)}, f32[5,512,128]{2,0,1:T(8,128)S(1)}, pred[512,4]{1,0:T(8,128)(4,1)S(1)}, /*index=5*/s32[512,4]{1,0:T(8,128)S(1)}, s32[]{:T(128)}) while((s32[]{:T(128)}, f32[16,32,128]{2,1,0:T(8,128)}, s32[16]{0:T(128)S(1)}, f32[5,512,128]{2,0,1:T(8,128)S(1)}, ...), condition=%wide.region_42.43_spmd, body=%wide.region_40.42_spmd.sunk | while | flops 37927808 | bytes 3855557 | solution.py:121
  283.8 10.9 %select_reduce_fusion.3 = f32[32,128]{1,0:T(8,128)S(1)} fusion(f32[32,512]{1,0:T(8,128)S(1)} %sub.2333, f32[32,128]{1,0:T(8,128)S(1)} %bitcast.362, f32[32,512]{1,0:T(8,128)S(1)} %sub.2334, f32[32,128]{1,0:T(8,128)S(1)} %bitcast.363, f32[32,512]{1,0:T(8,128)S(1)} %sub.2335, f32[32,128]{1,0:T(8,128)S(1)} %bitcast.364, f32[32,512]{1,0:T(8,128)S(1)} %add.1014, ...), kind=kLoop, calls=%fused_computation.609.clone.1 | loop fusion | flops 37744640 | bytes 507904 | tf_op jit(solution)/shard_map/while/body/eval_jaxpr/reduce_sum | solution.py:91
  302.5 10.9 %select_reduce_fusion.3 = f32[32,128]{1,0:T(8,128)S(1)} fusion(f32[32,512]{1,0:T(8,128)S(1)} %sub.2333, f32[32,128]{1,0:T(8,128)S(1)} %bitcast.362, f32[32,512]{1,0:T(8,128)S(1)} %sub.2334, f32[32,128]{1,0:T(8,128)S(1)} %bitcast.363, f32[32,512]{1,0:T(8,128)S(1)} %sub.2335, f32[32,128]{1,0:T(8,128)S(1)} %bitcast.364, f32[32,512]{1,0:T(8,128)S(1)} %add.1014, ...), kind=kLoop, calls=%fused_computation.609.clone.1 | loop fusion | flops 37744640 | bytes 507904 | tf_op jit(solution)/shard_map/while/body/eval_jaxpr/reduce_sum | solution.py:91
  321.1 10.9 %select_reduce_fusion.3 = f32[32,128]{1,0:T(8,128)S(1)} fusion(f32[32,512]{1,0:T(8,128)S(1)} %sub.2333, f32[32,128]{1,0:T(8,128)S(1)} %bitcast.362, f32[32,512]{1,0:T(8,128)S(1)} %sub.2334, f32[32,128]{1,0:T(8,128)S(1)} %bitcast.363, f32[32,512]{1,0:T(8,128)S(1)} %sub.2335, f32[32,128]{1,0:T(8,128)S(1)} %bitcast.364, f32[32,512]{1,0:T(8,128)S(1)} %add.1014, ...), kind=kLoop, calls=%fused_computation.609.clone.1 | loop fusion | flops 37744640 | bytes 507904 | tf_op jit(solution)/shard_map/while/body/eval_jaxpr/reduce_sum | solution.py:91
  339.7 10.9 %select_reduce_fusion.3 = f32[32,128]{1,0:T(8,128)S(1)} fusion(f32[32,512]{1,0:T(8,128)S(1)} %sub.2333, f32[32,128]{1,0:T(8,128)S(1)} %bitcast.362, f32[32,512]{1,0:T(8,128)S(1)} %sub.2334, f32[32,128]{1,0:T(8,128)S(1)} %bitcast.363, f32[32,512]{1,0:T(8,128)S(1)} %sub.2335, f32[32,128]{1,0:T(8,128)S(1)} %bitcast.364, f32[32,512]{1,0:T(8,128)S(1)} %add.1014, ...), kind=kLoop, calls=%fused_computation.609.clone.1 | loop fusion | flops 37744640 | bytes 507904 | tf_op jit(solution)/shard_map/while/body/eval_jaxpr/reduce_sum | solution.py:91
  358.4 10.9 %select_reduce_fusion.3 = f32[32,128]{1,0:T(8,128)S(1)} fusion(f32[32,512]{1,0:T(8,128)S(1)} %sub.2333, f32[32,128]{1,0:T(8,128)S(1)} %bitcast.362, f32[32,512]{1,0:T(8,128)S(1)} %sub.2334, f32[32,128]{1,0:T(8,128)S(1)} %bitcast.363, f32[32,512]{1,0:T(8,128)S(1)} %sub.2335, f32[32,128]{1,0:T(8,128)S(1)} %bitcast.364, f32[32,512]{1,0:T(8,128)S(1)} %add.1014, ...), kind=kLoop, calls=%fused_computation.609.clone.1 | loop fusion | flops 37744640 | bytes 507904 | tf_op jit(solution)/shard_map/while/body/eval_jaxpr/reduce_sum | solution.py:91
  377.0 10.9 %select_reduce_fusion.3 = f32[32,128]{1,0:T(8,128)S(1)} fusion(f32[32,512]{1,0:T(8,128)S(1)} %sub.2333, f32[32,128]{1,0:T(8,128)S(1)} %bitcast.362, f32[32,512]{1,0:T(8,128)S(1)} %sub.2334, f32[32,128]{1,0:T(8,128)S(1)} %bitcast.363, f32[32,512]{1,0:T(8,128)S(1)} %sub.2335, f32[32,128]{1,0:T(8,128)S(1)} %bitcast.364, f32[32,512]{1,0:T(8,128)S(1)} %add.1014, ...), kind=kLoop, calls=%fused_computation.609.clone.1 | loop fusion | flops 37744640 | bytes 507904 | tf_op jit(solution)/shard_map/while/body/eval_jaxpr/reduce_sum | solution.py:91
  395.6 10.9 %select_reduce_fusion.3 = f32[32,128]{1,0:T(8,128)S(1)} fusion(f32[32,512]{1,0:T(8,128)S(1)} %sub.2333, f32[32,128]{1,0:T(8,128)S(1)} %bitcast.362, f32[32,512]{1,0:T(8,128)S(1)} %sub.2334, f32[32,128]{1,0:T(8,128)S(1)} %bitcast.363, f32[32,512]{1,0:T(8,128)S(1)} %sub.2335, f32[32,128]{1,0:T(8,128)S(1)} %bitcast.364, f32[32,512]{1,0:T(8,128)S(1)} %add.1014, ...), kind=kLoop, calls=%fused_computation.609.clone.1 | loop fusion | flops 37744640 | bytes 507904 | tf_op jit(solution)/shard_map/while/body/eval_jaxpr/reduce_sum | solution.py:91
  414.3 10.9 %select_reduce_fusion.3 = f32[32,128]{1,0:T(8,128)S(1)} fusion(f32[32,512]{1,0:T(8,128)S(1)} %sub.2333, f32[32,128]{1,0:T(8,128)S(1)} %bitcast.362, f32[32,512]{1,0:T(8,128)S(1)} %sub.2334, f32[32,128]{1,0:T(8,128)S(1)} %bitcast.363, f32[32,512]{1,0:T(8,128)S(1)} %sub.2335, f32[32,128]{1,0:T(8,128)S(1)} %bitcast.364, f32[32,512]{1,0:T(8,128)S(1)} %add.1014, ...), kind=kLoop, calls=%fused_computation.609.clone.1 | loop fusion | flops 37744640 | bytes 507904 | tf_op jit(solution)/shard_map/while/body/eval_jaxpr/reduce_sum | solution.py:91
  432.9 10.9 %select_reduce_fusion.3 = f32[32,128]{1,0:T(8,128)S(1)} fusion(f32[32,512]{1,0:T(8,128)S(1)} %sub.2333, f32[32,128]{1,0:T(8,128)S(1)} %bitcast.362, f32[32,512]{1,0:T(8,128)S(1)} %sub.2334, f32[32,128]{1,0:T(8,128)S(1)} %bitcast.363, f32[32,512]{1,0:T(8,128)S(1)} %sub.2335, f32[32,128]{1,0:T(8,128)S(1)} %bitcast.364, f32[32,512]{1,0:T(8,128)S(1)} %add.1014, ...), kind=kLoop, calls=%fused_computation.609.clone.1 | loop fusion | flops 37744640 | bytes 507904 | tf_op jit(solution)/shard_map/while/body/eval_jaxpr/reduce_sum | solution.py:91
  451.5 10.9 %select_reduce_fusion.3 = f32[32,128]{1,0:T(8,128)S(1)} fusion(f32[32,512]{1,0:T(8,128)S(1)} %sub.2333, f32[32,128]{1,0:T(8,128)S(1)} %bitcast.362, f32[32,512]{1,0:T(8,128)S(1)} %sub.2334, f32[32,128]{1,0:T(8,128)S(1)} %bitcast.363, f32[32,512]{1,0:T(8,128)S(1)} %sub.2335, f32[32,128]{1,0:T(8,128)S(1)} %bitcast.364, f32[32,512]{1,0:T(8,128)S(1)} %add.1014, ...), kind=kLoop, calls=%fused_computation.609.clone.1 | loop fusion | flops 37744640 | bytes 507904 | tf_op jit(solution)/shard_map/while/body/eval_jaxpr/reduce_sum | solution.py:91
  470.2 10.9 %select_reduce_fusion.3 = f32[32,128]{1,0:T(8,128)S(1)} fusion(f32[32,512]{1,0:T(8,128)S(1)} %sub.2333, f32[32,128]{1,0:T(8,128)S(1)} %bitcast.362, f32[32,512]{1,0:T(8,128)S(1)} %sub.2334, f32[32,128]{1,0:T(8,128)S(1)} %bitcast.363, f32[32,512]{1,0:T(8,128)S(1)} %sub.2335, f32[32,128]{1,0:T(8,128)S(1)} %bitcast.364, f32[32,512]{1,0:T(8,128)S(1)} %add.1014, ...), kind=kLoop, calls=%fused_computation.609.clone.1 | loop fusion | flops 37744640 | bytes 507904 | tf_op jit(solution)/shard_map/while/body/eval_jaxpr/reduce_sum | solution.py:91
  488.8 10.9 %select_reduce_fusion.3 = f32[32,128]{1,0:T(8,128)S(1)} fusion(f32[32,512]{1,0:T(8,128)S(1)} %sub.2333, f32[32,128]{1,0:T(8,128)S(1)} %bitcast.362, f32[32,512]{1,0:T(8,128)S(1)} %sub.2334, f32[32,128]{1,0:T(8,128)S(1)} %bitcast.363, f32[32,512]{1,0:T(8,128)S(1)} %sub.2335, f32[32,128]{1,0:T(8,128)S(1)} %bitcast.364, f32[32,512]{1,0:T(8,128)S(1)} %add.1014, ...), kind=kLoop, calls=%fused_computation.609.clone.1 | loop fusion | flops 37744640 | bytes 507904 | tf_op jit(solution)/shard_map/while/body/eval_jaxpr/reduce_sum | solution.py:91
  507.4 10.9 %select_reduce_fusion.3 = f32[32,128]{1,0:T(8,128)S(1)} fusion(f32[32,512]{1,0:T(8,128)S(1)} %sub.2333, f32[32,128]{1,0:T(8,128)S(1)} %bitcast.362, f32[32,512]{1,0:T(8,128)S(1)} %sub.2334, f32[32,128]{1,0:T(8,128)S(1)} %bitcast.363, f32[32,512]{1,0:T(8,128)S(1)} %sub.2335, f32[32,128]{1,0:T(8,128)S(1)} %bitcast.364, f32[32,512]{1,0:T(8,128)S(1)} %add.1014, ...), kind=kLoop, calls=%fused_computation.609.clone.1 | loop fusion | flops 37744640 | bytes 507904 | tf_op jit(solution)/shard_map/while/body/eval_jaxpr/reduce_sum | solution.py:91
  526.0 10.9 %select_reduce_fusion.3 = f32[32,128]{1,0:T(8,128)S(1)} fusion(f32[32,512]{1,0:T(8,128)S(1)} %sub.2333, f32[32,128]{1,0:T(8,128)S(1)} %bitcast.362, f32[32,512]{1,0:T(8,128)S(1)} %sub.2334, f32[32,128]{1,0:T(8,128)S(1)} %bitcast.363, f32[32,512]{1,0:T(8,128)S(1)} %sub.2335, f32[32,128]{1,0:T(8,128)S(1)} %bitcast.364, f32[32,512]{1,0:T(8,128)S(1)} %add.1014, ...), kind=kLoop, calls=%fused_computation.609.clone.1 | loop fusion | flops 37744640 | bytes 507904 | tf_op jit(solution)/shard_map/while/body/eval_jaxpr/reduce_sum | solution.py:91
  544.7 10.9 %select_reduce_fusion.3 = f32[32,128]{1,0:T(8,128)S(1)} fusion(f32[32,512]{1,0:T(8,128)S(1)} %sub.2333, f32[32,128]{1,0:T(8,128)S(1)} %bitcast.362, f32[32,512]{1,0:T(8,128)S(1)} %sub.2334, f32[32,128]{1,0:T(8,128)S(1)} %bitcast.363, f32[32,512]{1,0:T(8,128)S(1)} %sub.2335, f32[32,128]{1,0:T(8,128)S(1)} %bitcast.364, f32[32,512]{1,0:T(8,128)S(1)} %add.1014, ...), kind=kLoop, calls=%fused_computation.609.clone.1 | loop fusion | flops 37744640 | bytes 507904 | tf_op jit(solution)/shard_map/while/body/eval_jaxpr/reduce_sum | solution.py:91
  563.3 10.9 %select_reduce_fusion.3 = f32[32,128]{1,0:T(8,128)S(1)} fusion(f32[32,512]{1,0:T(8,128)S(1)} %sub.2333, f32[32,128]{1,0:T(8,128)S(1)} %bitcast.362, f32[32,512]{1,0:T(8,128)S(1)} %sub.2334, f32[32,128]{1,0:T(8,128)S(1)} %bitcast.363, f32[32,512]{1,0:T(8,128)S(1)} %sub.2335, f32[32,128]{1,0:T(8,128)S(1)} %bitcast.364, f32[32,512]{1,0:T(8,128)S(1)} %add.1014, ...), kind=kLoop, calls=%fused_computation.609.clone.1 | loop fusion | flops 37744640 | bytes 507904 | tf_op jit(solution)/shard_map/while/body/eval_jaxpr/reduce_sum | solution.py:91
  574.8 7.6 %all-to-all-start.2 = ((f32[16,32,128]{2,1,0:T(8,128)}), f32[16,32,128]{2,1,0:T(8,128)S(1)}, u32[]{:S(2)}, u32[]{:S(2)}) async-start(f32[16,32,128]{2,1,0:T(8,128)} %get-tuple-element.182), calls=%async_computation.2 | async-start | bytes 524288 | tf_op jit(solution)/shard_map/all_to_all | solution.py:150
  582.5 8.5 %all-to-all-done.2 = f32[16,32,128]{2,1,0:T(8,128)S(1)} async-done(((f32[16,32,128]{2,1,0:T(8,128)}), f32[16,32,128]{2,1,0:T(8,128)S(1)}, u32[]{:S(2)}, u32[]{:S(2)}) %all-to-all-start.2) | async-done | bytes 262176 | tf_op jit(solution)/shard_map/all_to_all | solution.py:150
  (1465 shorter events, 319.7 us)
Async XLA Ops:
  7.2 15.1 %copy-start.1 = (f32[3,32768]{1,0:T(4,128)S(1)}, f32[3,32768]{1,0:T(4,128)}, u32[]{:S(2)}) copy-start(f32[3,32768]{1,0:T(4,128)} %param.9) | copy-start | bytes 1179652
  7.2 15.2 %copy-start.2 = (f32[64]{0:T(128)S(1)}, f32[64]{0:T(128)}, u32[]{:S(2)}) copy-start(f32[64]{0:T(128)} %param.10) | copy-start | bytes 772
  15.0 210.9 %all-to-all-start.1 = ((f32[1,16,32]{2,0,1:T(1,128)}), f32[1,16,32]{2,0,1:T(1,128)S(1)}, u32[]{:S(2)}, u32[]{:S(2)}) async-start(f32[1,16,32]{2,0,1:T(1,128)} %bitcast.79), calls=%async_computation.1 | async-start | bytes 16384 | tf_op jit(solution)/shard_map/all_to_all | solution.py:146
  22.2 252.6 %top_k.23.cloned.1.call-start = ((), (), s32[]{:S(2)}) async-start(), calls=%async_computation.3 | async-start | bytes 6291488 | tf_op jit(solution)/shard_map/top_k | solution.py:102
  223.1 1.0 copy-start
  233.0 43.8 %all-to-all-start = ((f32[5,512,128]{2,0,1:T(8,128)}), f32[5,512,128]{2,0,1:T(8,128)S(1)}, u32[]{:S(2)}, u32[]{:S(2)}) async-start(f32[5,512,128]{2,0,1:T(8,128)} %select_bitcast_fusion.2), calls=%async_computation | async-start | bytes 4194304 | tf_op jit(solution)/shard_map/all_to_all | solution.py:145
  574.8 16.1 %all-to-all-start.2 = ((f32[16,32,128]{2,1,0:T(8,128)}), f32[16,32,128]{2,1,0:T(8,128)S(1)}, u32[]{:S(2)}, u32[]{:S(2)}) async-start(f32[16,32,128]{2,1,0:T(8,128)} %get-tuple-element.182), calls=%async_computation.2 | async-start | bytes 524288 | tf_op jit(solution)/shard_map/all_to_all | solution.py:150
Sparse Core Ops, SparseCore 0:
  229.7 44.7 top_k.25.cloned.1.call-done
  (1 shorter events, 0.0 us)
where the time goes:
time: 601 us; the launch traced here: 599 us
  other arithmetic  310 us (52%)
  local copies, waits for them, and re-layouts  127 us (21%)
  matrix products  109 us (18%)
  starting transfers between devices  21.9 us (4%)
  between operations  14.2 us (2%)
  loops' own time  9.35 us (2%)
  waiting for transfers between devices  8.49 us (1%)
    reduce_sum x16, other arithmetic, tile_rates(): return own_rows[4] * jnp.sum(pair_term, axis=2) / span_width  174 us
    dot_general x128, matrix products, propagate(): jnp.dot(density_table[None, :], hat_weights, precision=lax.Precision.HIGH...  109 us
    top_k x4, local copies, waits for them, and re-layouts, find_partners(): values, partners = lax.top_k(scores, MOST)  36.7 us
    reduce_sum x120, other arithmetic, propagate(): radius_sq = jnp.sum(position * position, axis=0)  28.7 us
    sub x128, other arithmetic, propagate(): 1.0 - 5.0 * polar_ratio  19 us
    reduce_sum x128, other arithmetic, propagate(): air_speed = jnp.sqrt(jnp.sum(relative * relative, axis=0))  18.4 us
    slice x16, local copies, waits for them, and re-layouts, tile_rates(): mate_rows[4][:, None, :]  14.4 us
    gather x16, local copies, waits for them, and re-layouts, one_group(): jnp.take(received, group_mates.reshape(group_size * MOST), axis=1)  12.2 us
  transfers between devices with their start and end apart: 3, of which 1 were waited for; matrix products, arithmetic and copies ran while one was open for 33% of the time, Pallas kernels for 0%

commit v1 on v0

v1 whole, which is shorter than its diff:
```python
import functools

import jax
import jax.numpy as jnp
from jax import lax
from jax.experimental import pallas as pl
from jax.experimental.pallas import tpu as pltpu
from jax.sharding import PartitionSpec as P

F32 = jnp.float32
BF16 = jnp.bfloat16
BLK = 128
NB = 256
NS = 16
CAP = 32
SLOTS = NS * CAP
CUBES = 128
MOST = 4
SUB = 16
ROWS = 5 * CAP + 8
KF = 32
PITCH = SLOTS + 8

TIME_STEP = 0.2
EARTH_SPIN = 0.0588
J2_COEF = 0.00108263
DRAG_SCALE = 0.008
TABLE_SCALE = 63 / 0.4
SPEED_FLOOR = 0.04


def iota(shape, dim):
    return lax.broadcasted_iota(jnp.int32, shape, dim)


def split2(x):
    high = x.astype(BF16)
    return high, (x - high.astype(F32)).astype(BF16)


def columns_of(row):
    parts = [
        jnp.transpose(jnp.broadcast_to(row[:, k : k + BLK], (BLK, BLK)))
        for k in range(0, row.shape[1], BLK)
    ]
    return jnp.concatenate(parts, axis=0)


def rank_row(row):
    n = row.shape[1]
    column = columns_of(row)
    ranks = []
    for k in range(0, n, BLK):
        earlier = iota((n, BLK), 0) < iota((n, BLK), 1) + k
        same = column == row[:, k : k + BLK]
        ranks.append(jnp.sum(jnp.where(earlier & same, 1.0, 0.0), axis=0, keepdims=True))
    return jnp.concatenate(ranks, axis=1)


def block_slots(cube_row):
    owner = lax.shift_right_logical(cube_row, 7).astype(F32)
    return owner * CAP + rank_row(owner)


def substep(x, y, z, vx, vy, vz, drag, tab, slope):
    r2 = x * x + y * y + z * z
    ri = lax.rsqrt(r2)
    h = r2 * ri - 1.0
    coord = jnp.clip(h * TABLE_SCALE, -1.0, 64.0)
    below = jnp.floor(coord)
    frac = coord - below
    index = below.astype(jnp.int32) + 1
    base = jnp.concatenate(
        [jnp.take_along_axis(tab, index[k : k + 8], axis=1) for k in range(0, x.shape[0], 8)], axis=0
    )
    rise = jnp.concatenate(
        [jnp.take_along_axis(slope, index[k : k + 8], axis=1) for k in range(0, x.shape[0], 8)], axis=0
    )
    density = jnp.exp(base + frac * rise - h * 10.0)
    ux = vx + EARTH_SPIN * y
    uy = vy - EARTH_SPIN * x
    u2 = ux * ux + uy * uy + vz * vz
    speed = u2 * lax.rsqrt(jnp.maximum(u2, 1e-36))
    pull = density * drag * speed
    i2 = ri * ri
    i3 = i2 * ri
    oblate = (1.5 * J2_COEF * TIME_STEP) * (i2 * i3)
    near = TIME_STEP * i3 + oblate * (1.0 - 5.0 * (z * z * i2))
    vx = vx - x * near - pull * ux
    vy = vy - y * near - pull * uy
    vz = vz - z * (near + 2.0 * oblate) - pull * vz
    return x + TIME_STEP * vx, y + TIME_STEP * vy, z + TIME_STEP * vz, vx, vy, vz


def propagate_kernel(chunk, orbit, props, table, cube, next_out, send, rows, prows, state, planes):
    def spread(b, carry):
        col = pl.ds(pl.multiple_of(b * BLK, BLK), BLK)
        at = pl.multiple_of(b * 8, 8)
        rows[pl.ds(at, 6), :] = orbit[:, col]
        prows[pl.ds(at, 3), :] = props[:, col]
        return carry

    lax.fori_loop(0, NB, spread, 0, unroll=8)

    tab = jnp.concatenate([table[...], jnp.zeros((1, 64), F32)], axis=1)
    tab = pltpu.roll(jnp.broadcast_to(tab, (8, BLK)), 1, 1)
    slope = pltpu.roll(tab, BLK - 1, 1) - tab

    def advance(g, carry):
        def load(ref, c):
            return jnp.concatenate(
                [
                    ref[pl.ds(g * (chunk * 8) + k * 8 + c, 8, stride=8), :]
                    for k in range(0, chunk, 8)
                ],
                axis=0,
            )

        at = pl.ds(pl.multiple_of(g * chunk, chunk), chunk)
        now = tuple(load(rows, c) for c in range(6))
        drag = load(prows, 2) * (DRAG_SCALE * TIME_STEP)
        planes[3, at, :] = load(prows, 0)
        planes[4, at, :] = load(prows, 1)
        now = lax.fori_loop(0, SUB, lambda s, v: substep(*v, drag, tab, slope), now, unroll=2)
        for c in range(6):
            for k in range(0, chunk, 8):
                rows[pl.ds(g * (chunk * 8) + k * 8 + c, 8, stride=8), :] = now[c][k : k + 8]
        for c in range(3):
            planes[c, at, :] = now[3 + c]
        return carry

    lax.fori_loop(0, NB // chunk, advance, 0)

    def collect(b, carry):
        col = pl.ds(pl.multiple_of(b * BLK, BLK), BLK)
        next_out[:, col] = rows[pl.ds(pl.multiple_of(b * 8, 8), 6), :]
        return carry

    lax.fori_loop(0, NB, collect, 0, unroll=8)

    slot = block_slots(cube[...])
    pick = jnp.where(slot == iota((SLOTS, NB), 0).astype(F32), 1.0, 0.0).astype(BF16)
    for c in range(5):
        high, low = split2(planes[c])
        got = jnp.dot(pick, jnp.concatenate([high, low], axis=1), preferred_element_type=F32)
        send[:, c * CAP : (c + 1) * CAP, :] = (got[:, :BLK] + got[:, BLK:]).reshape(NS, CAP, BLK)
    local = ((cube[...] & (CUBES - 1)) + 1).astype(F32)
    ids = jnp.dot(pick, columns_of(local).astype(BF16), preferred_element_type=F32)
    id_rows = []
    for q in range(SLOTS // BLK):
        line = jnp.transpose(ids[q * BLK : (q + 1) * BLK])[0:1]
        id_rows.append(jnp.broadcast_to(line, (4, BLK)))
    id_rows = jnp.concatenate(id_rows, axis=0)
    mine = lax.shift_right_logical(iota((NS, BLK), 1), 5) == (iota((NS, BLK), 0) & 3)
    id_rows = jnp.where(mine, id_rows, 0.0)
    id_rows = id_rows + pltpu.roll(id_rows, 64, 1)
    id_rows = id_rows + pltpu.roll(id_rows, 32, 1)
    send[:, 5 * CAP :, :] = jnp.broadcast_to(id_rows[:, None, :], (NS, 8, BLK))


def features(planes):
    v, (rh, rm), (wh, wm) = planes[:3], planes[3], planes[4]
    radius, weight = rh + rm, wh + wm
    full = [h + m for h, m in v]
    norm = full[0] * full[0] + full[1] * full[1] + full[2] * full[2]

    def thirds(x):
        a = x.astype(BF16).astype(F32)
        b = (x - a).astype(BF16).astype(F32)
        return [a, b, x - a - b]

    one = jnp.ones_like(radius)
    left, right = [], []
    for h, m in v:
        left += [h, h, m, m]
        right += [-2.0 * h, -2.0 * m, -2.0 * h, -2.0 * m]
    left += thirds(norm) + [one, one, one]
    right += [one, one, one] + thirds(norm + SPEED_FLOOR)
    p, q, t = weight, weight * radius, weight * radius * radius

    def halves(x):
        a = x.astype(BF16).astype(F32)
        return a, x - a

    (ph, pm), (qh, qm), (th, tm) = halves(p), halves(q), halves(t)
    left += [th, th, tm, 2.0 * qh, 2.0 * qh, 2.0 * qm, ph, ph, pm]
    right += [ph, pm, ph, qh, qm, qh, th, tm, th]
    return left, right


def pair_kernel(recv, back, left, right, rate):
    got = recv[:, 5 * CAP, :]
    mine = lax.shift_right_logical(iota((NS, BLK), 1), 5) == (iota((NS, BLK), 0) & 3)
    got = jnp.where(mine, got, 0.0)
    ids = jnp.concatenate(
        [jnp.sum(got[4 * q : 4 * q + 4], axis=0, keepdims=True) for q in range(4)], axis=1
    )
    place = jnp.where(ids > 0.0, (ids - 1.0) * MOST + rank_row(ids), -1.0)
    pick = jnp.where(place == iota((SLOTS, SLOTS), 0).astype(F32), 1.0, 0.0).astype(BF16)
    planes = []
    for c in range(5):
        plane = recv[:, c * CAP : (c + 1) * CAP, :].reshape(SLOTS, BLK)
        high, low = split2(plane)
        out = jnp.dot(pick, jnp.concatenate([high, low], axis=1), preferred_element_type=F32)
        planes.append((out[:, :BLK], out[:, BLK:]))
    lefts, rights = features(planes)
    zero = jnp.zeros((SLOTS, BLK), F32)
    for f in range(KF):
        left[f * PITCH : f * PITCH + SLOTS, :] = lefts[f] if f < len(lefts) else zero
        right[f * PITCH : f * PITCH + SLOTS, :] = rights[f] if f < len(rights) else zero

    gap_rows = iota((KF, BLK), 0) < 18
    off_diag = iota((BLK, BLK), 0) != iota((BLK, BLK), 1)

    def one_cube(q):
        base = q * MOST
        lhs = jnp.concatenate(
            [left[pl.ds(base + m, KF, stride=PITCH), :].astype(BF16) for m in range(MOST)], axis=1
        )
        row_sums = [None] * MOST
        out = []
        for c in range(MOST):
            r = right[pl.ds(base + c, KF, stride=PITCH), :]
            rhs = jnp.concatenate(
                [jnp.where(gap_rows, r, 0.0), jnp.where(gap_rows, 0.0, r)], axis=1
            ).astype(BF16)
            tiles = lax.dot_general(
                lhs[:, : (c + 1) * BLK], rhs, (((0,), (0,)), ((), ())), preferred_element_type=F32
            )
            total = None
            for a in range(c + 1):
                gap = jnp.maximum(tiles[a * BLK : (a + 1) * BLK, :BLK], SPEED_FLOOR)
                pair = tiles[a * BLK : (a + 1) * BLK, BLK:] * (gap * lax.rsqrt(gap))
                if a == c:
                    pair = jnp.where(off_diag, pair, 0.0)
                else:
                    row_sums[a] = pair if row_sums[a] is None else row_sums[a] + pair
                part = jnp.sum(pair.reshape(16, 8, BLK), axis=0)
                total = part if total is None else total + part
            out.append(total)
        for c in range(MOST):
            total = out[c]
            if row_sums[c] is not None:
                total = total + jnp.sum(jnp.transpose(row_sums[c]).reshape(16, 8, BLK), axis=0)
            rate[pl.ds(base + c, 1), :] = jnp.sum(total, axis=0, keepdims=True) * (1.0 / (MOST * BLK))

    def cubes(q, carry):
        one_cube(q)
        return carry

    lax.fori_loop(0, CUBES, cubes, 0)

    place_col = columns_of(place)
    unpick = jnp.concatenate(
        [
            jnp.where(place_col == (iota((SLOTS, BLK), 1) + k).astype(F32), 1.0, 0.0)
            for k in range(0, SLOTS, BLK)
        ],
        axis=1,
    ).astype(BF16)
    high, low = split2(rate[...])
    out = jnp.dot(unpick, jnp.concatenate([high, low], axis=1), preferred_element_type=F32)
    back[...] = (out[:, :BLK] + out[:, BLK:]).reshape(NS, CAP, BLK)


def unpack_kernel(back, cube, out):
    slot_col = columns_of(block_slots(cube[...]))
    pick = jnp.concatenate(
        [
            jnp.where(slot_col == (iota((NB, BLK), 1) + k).astype(F32), 1.0, 0.0)
            for k in range(0, SLOTS, BLK)
        ],
        axis=1,
    ).astype(BF16)
    high, low = split2(back[...].reshape(SLOTS, BLK))
    got = jnp.dot(pick, jnp.concatenate([high, low], axis=1), preferred_element_type=F32)
    out[...] = got[:, :BLK] + got[:, BLK:]


VMEM = pl.BlockSpec(memory_space=pltpu.VMEM)
PARAMS = pltpu.CompilerParams(vmem_limit_bytes=56 * 2**20)


def propagate_call(orbit_state, object_props, table, cube, chunk=32):
    return pl.pallas_call(
        functools.partial(propagate_kernel, chunk),
        out_shape=(
            jax.ShapeDtypeStruct((6, NB * BLK), F32),
            jax.ShapeDtypeStruct((NS, ROWS, BLK), F32),
        ),
        in_specs=[VMEM] * 4,
        out_specs=(VMEM, VMEM),
        scratch_shapes=[
            pltpu.VMEM((NB * 8, BLK), F32),
            pltpu.VMEM((NB * 8, BLK), F32),
            pltpu.VMEM((8, BLK), F32),
            pltpu.VMEM((5, NB, BLK), F32),
        ],
        compiler_params=PARAMS,
        name="propagate",
    )(orbit_state, object_props, table, cube)


def pair_call(recv):
    return pl.pallas_call(
        pair_kernel,
        out_shape=jax.ShapeDtypeStruct((NS, CAP, BLK), F32),
        in_specs=[VMEM],
        out_specs=VMEM,
        scratch_shapes=[
            pltpu.VMEM((KF * PITCH, BLK), F32),
            pltpu.VMEM((KF * PITCH, BLK), F32),
            pltpu.VMEM((SLOTS, BLK), F32),
        ],
        compiler_params=PARAMS,
        name="pairs",
    )(recv)


def unpack_call(back, cube):
    return pl.pallas_call(
        unpack_kernel,
        out_shape=jax.ShapeDtypeStruct((NB, BLK), F32),
        in_specs=[VMEM] * 2,
        out_specs=VMEM,
        compiler_params=PARAMS,
        name="unpack",
    )(back, cube)


def on_device(orbit_state, object_props, density_table, block_cube):
    cube = block_cube.reshape(1, NB)
    next_state, send = propagate_call(orbit_state, object_props, density_table.reshape(1, 64), cube)
    recv = lax.all_to_all(send, "space", split_axis=0, concat_axis=0, tiled=True)
    back = pair_call(recv)
    home = lax.all_to_all(back, "space", split_axis=0, concat_axis=0, tiled=True)
    return next_state, unpack_call(home, cube).reshape(NB * BLK)


def solution(mesh):
    placed = (P(None, ("mc", "space")), P(None, ("mc", "space")), P(), P(("mc", "space")))
    return jax.shard_map(
        on_device,
        mesh=mesh,
        in_specs=placed,
        out_specs=(P(None, ("mc", "space")), P(("mc", "space"))),
        check_vma=False,
    )
```

time: 601 us -> 120 us (0.20)
  other arithmetic: 310 us -> 0 us
  local copies, waits for them, and re-layouts: 127 us -> 0 us
  matrix products: 109 us -> 0 us
  Pallas kernels: 0 us -> 79.1 us
  blocking collectives: 0 us -> 40.3 us
  starting transfers between devices: 21.9 us -> 0 us
  between operations: 14.2 us -> 0.63 us
  loops' own time: 9.35 us -> 0 us
  waiting for transfers between devices: 8.49 us -> 0 us
    reduce_sum x266 -> x0, other arithmetic: 221 us -> none  [the longest x16 174 us: tile_rates(): return own_rows[4] * jnp.sum(pair_term, axis=2) / span_width]
    dot_general x128 -> x0, matrix products: 109 us -> none  [propagate(): jnp.dot(density_table[None, :], hat_weights, precision=lax.Precision.HIGH...]
    pallas_call x0 -> x3, Pallas kernels: none -> 79.1 us  [the longest x1 57 us: pair_call(): pl.pallas_call(pair_kernel, out_shape=jax.ShapeDtypeStruct((NS, CAP, BLK)...]
    gather x68 -> x0, local copies, waits for them, and re-layouts: 46.5 us -> none  [the longest x16 12.2 us: one_group(): jnp.take(received, group_mates.reshape(group_size * MOST), axis=1)]
    all_to_all x0 -> x2, blocking collectives: none -> 40.3 us  [the longest x1 27.6 us: on_device(): lax.all_to_all(send, 'space', split_axis=0, concat_axis=0, tiled=True)]
    top_k x4 -> x0, local copies, waits for them, and re-layouts: 36.7 us -> none  [find_partners(): values, partners = lax.top_k(scores, MOST)]
    add x32 -> x0, other arithmetic: 22.2 us -> none  [the longest x8 10.6 us: propagate(): velocity[0] + EARTH_SPIN * position[1]]
    all_to_all x3 -> x0, starting transfers between devices: 21.9 us -> none  [the longest x1 7.58 us: on_device(): lax.all_to_all(block_rates, 'space', split_axis=0, concat_axis=0, tiled=T...]
  transfers between devices with their start and end apart: 3 -> 0, of which waited for: 1 -> 0; matrix products, arithmetic and copies ran while one was open for 33% -> 0% of each run, Pallas kernels for 0% -> 0%
where the time goes in v1:
time: 120 us
  Pallas kernels  79.1 us (66%)
  blocking collectives  40.3 us (34%)
    pallas_call x1, Pallas kernels, pair_call(): pl.pallas_call(pair_kernel, out_shape=jax.ShapeDtypeStruct((NS, CAP, BLK)...  57 us
    all_to_all x1, blocking collectives, on_device(): lax.all_to_all(send, 'space', split_axis=0, concat_axis=0, tiled=True)  27.6 us
    pallas_call x1, Pallas kernels, propagate_call(): pl.pallas_call(functools.partial(propagate_kernel, chunk), out_shape=(jax...  20.2 us
    all_to_all x1, blocking collectives, on_device(): lax.all_to_all(back, 'space', split_axis=0, concat_axis=0, tiled=True)  12.7 us

profile of v1, /device:TPU:0, one launch (start us, length us, event | category | flops | bytes accessed | tf_op | source)
XLA Modules:
  0.0 120.1 jit_solution(11676996089608409745)
XLA Ops:
  0.6 20.2 %propagate.1 = (f32[6,32768]{1,0:T(8,128)}, f32[16,168,128]{2,1,0:T(8,128)}) custom-call(f32[6,32768]{1,0:T(8,128)} %orbit.1, f32[3,32768]{1,0:T(4,128)} %props.1, f32[1,64]{1,0:T(1,128)} %bitcast.6, s32[1,256]{1,0:T(1,128)} %bitcast.4), custom_call_target="tpu_custom_call" | custom-call | tf_op jit(solution)/shard_map/propagate/pallas_call | solution.py:285
  20.8 27.6 %all_to_all.10.recv = f32[16,168,128]{2,1,0:T(8,128)} all-to-all(f32[16,168,128]{2,1,0:T(8,128)} %get-tuple-element.5), channel_id=1, replica_groups=mesh['mc'=8,'space'=16] {'space'}, dimensions={0} | all-to-all | bytes 2752512 | tf_op jit(solution)/shard_map/all_to_all | solution.py:334
  48.4 57.0 %pairs.1 = f32[16,32,128]{2,1,0:T(8,128)} custom-call(f32[16,168,128]{2,1,0:T(8,128)} %all_to_all.10.recv), custom_call_target="tpu_custom_call" | custom-call | tf_op jit(solution)/shard_map/pairs/pallas_call | solution.py:305
  105.4 12.7 %all_to_all.11.back = f32[16,32,128]{2,1,0:T(8,128)} all-to-all(f32[16,32,128]{2,1,0:T(8,128)} %pairs.1), channel_id=1, replica_groups=mesh['mc'=8,'space'=16] {'space'}, dimensions={0} | all-to-all | bytes 524288 | tf_op jit(solution)/shard_map/all_to_all | solution.py:336
  118.0 2.0 %unpack.1 = f32[256,128]{1,0:T(8,128)} custom-call(f32[16,32,128]{2,1,0:T(8,128)} %all_to_all.11.back, s32[1,256]{1,0:T(1,128)} %bitcast.5), custom_call_target="tpu_custom_call" | custom-call | tf_op jit(solution)/shard_map/unpack/pallas_call | solution.py:321

commit v2 on v1

--- a/solution.py
+++ b/solution.py
@@ -248,7 +248,7 @@
         one_cube(q)
         return carry
 
-    lax.fori_loop(0, CUBES, cubes, 0)
+    lax.fori_loop(0, CUBES, cubes, 0, unroll=8)
 
     place_col = columns_of(place)
     unpick = jnp.concatenate(
@@ -281,7 +281,7 @@
 PARAMS = pltpu.CompilerParams(vmem_limit_bytes=56 * 2**20)
 
 
-def propagate_call(orbit_state, object_props, table, cube, chunk=32):
+def propagate_call(orbit_state, object_props, table, cube, chunk=256):
     return pl.pallas_call(
         functools.partial(propagate_kernel, chunk),
         out_shape=(

time: 120 us -> 85.4 us (0.71)
  Pallas kernels: 79.1 us -> 44.1 us
    pallas_call x1, Pallas kernels: 57 us -> 30.9 us  [pair_call(): pl.pallas_call(pair_kernel, out_shape=jax.ShapeDtypeStruct((NS, CAP, BLK)...]
    pallas_call x1, Pallas kernels: 20.2 us -> 11.2 us  [propagate_call(): pl.pallas_call(functools.partial(propagate_kernel, chunk), out_shape=(jax...]
where the time goes in v2:
time: 85.4 us; the launch traced here: 85 us
  Pallas kernels  44.1 us (52%)
  blocking collectives  40.3 us (47%)
    pallas_call x1, Pallas kernels, pair_call(): pl.pallas_call(pair_kernel, out_shape=jax.ShapeDtypeStruct((NS, CAP, BLK)...  30.9 us
    all_to_all x1, blocking collectives, on_device(): lax.all_to_all(send, 'space', split_axis=0, concat_axis=0, tiled=True)  27.6 us
    all_to_all x1, blocking collectives, on_device(): lax.all_to_all(back, 'space', split_axis=0, concat_axis=0, tiled=True)  12.7 us
    pallas_call x1, Pallas kernels, propagate_call(): pl.pallas_call(functools.partial(propagate_kernel, chunk), out_shape=(jax...  11.2 us
    pallas_call x1, Pallas kernels, unpack_call(): pl.pallas_call(unpack_kernel, out_shape=jax.ShapeDtypeStruct((NB, BLK), F...  2.02 us

profile of v2, /device:TPU:0, one launch (start us, length us, event | category | flops | bytes accessed | tf_op | source)
XLA Modules:
  0.0 85.0 jit_solution(2978369548991865097)
XLA Ops:
  0.6 11.2 %propagate.1 = (f32[6,32768]{1,0:T(8,128)}, f32[16,168,128]{2,1,0:T(8,128)}) custom-call(f32[6,32768]{1,0:T(8,128)} %orbit.1, f32[3,32768]{1,0:T(4,128)} %props.1, f32[1,64]{1,0:T(1,128)} %bitcast.6, s32[1,256]{1,0:T(1,128)} %bitcast.4), custom_call_target="tpu_custom_call" | custom-call | tf_op jit(solution)/shard_map/propagate/pallas_call | solution.py:285
  11.8 27.6 %all_to_all.10.recv = f32[16,168,128]{2,1,0:T(8,128)} all-to-all(f32[16,168,128]{2,1,0:T(8,128)} %get-tuple-element.5), channel_id=1, replica_groups=mesh['mc'=8,'space'=16] {'space'}, dimensions={0} | all-to-all | bytes 2752512 | tf_op jit(solution)/shard_map/all_to_all | solution.py:334
  39.4 30.9 %pairs.1 = f32[16,32,128]{2,1,0:T(8,128)} custom-call(f32[16,168,128]{2,1,0:T(8,128)} %all_to_all.10.recv), custom_call_target="tpu_custom_call" | custom-call | tf_op jit(solution)/shard_map/pairs/pallas_call | solution.py:305
  70.4 12.7 %all_to_all.11.back = f32[16,32,128]{2,1,0:T(8,128)} all-to-all(f32[16,32,128]{2,1,0:T(8,128)} %pairs.1), channel_id=1, replica_groups=mesh['mc'=8,'space'=16] {'space'}, dimensions={0} | all-to-all | bytes 524288 | tf_op jit(solution)/shard_map/all_to_all | solution.py:336
  83.0 2.0 %unpack.1 = f32[256,128]{1,0:T(8,128)} custom-call(f32[16,32,128]{2,1,0:T(8,128)} %all_to_all.11.back, s32[1,256]{1,0:T(1,128)} %bitcast.5), custom_call_target="tpu_custom_call" | custom-call | tf_op jit(solution)/shard_map/unpack/pallas_call | solution.py:321

commit v3 on v2

--- a/solution.py
+++ b/solution.py
@@ -1,5 +1,3 @@
-import functools
-
 import jax
 import jax.numpy as jnp
 from jax import lax
@@ -9,6 +7,7 @@
 
 F32 = jnp.float32
 BF16 = jnp.bfloat16
+MESH = pl.DeviceIdType.MESH
 BLK = 128
 NB = 256
 NS = 16
@@ -17,7 +16,7 @@
 CUBES = 128
 MOST = 4
 SUB = 16
-ROWS = 5 * CAP + 8
+GROUP = 8
 KF = 32
 PITCH = SLOTS + 8
 
@@ -57,9 +56,11 @@
     return jnp.concatenate(ranks, axis=1)
 
 
-def block_slots(cube_row):
-    owner = lax.shift_right_logical(cube_row, 7).astype(F32)
-    return owner * CAP + rank_row(owner)
+def cube_maps(cube_row):
+    low, high = cube_row & 15, lax.shift_right_logical(cube_row, 4)
+    spread = [(low + f) & 15 for f in (0, high, 5 * high + lax.shift_right_logical(high, 3))]
+    owner = lax.shift_right_logical(cube_row, 7)
+    return [(owner, cube_row & (CUBES - 1))] + [(to, high) for to in spread]
 
 
 def substep(x, y, z, vx, vy, vz, drag, tab, slope):
@@ -92,7 +93,80 @@
     return x + TIME_STEP * vx, y + TIME_STEP * vy, z + TIME_STEP * vz, vx, vy, vz
 
 
-def propagate_kernel(chunk, orbit, props, table, cube, next_out, send, rows, prows, state, planes):
+def hello(me):
+    barrier = pltpu.get_barrier_semaphore()
+
+    def tell(k, carry):
+        pl.semaphore_signal(
+            barrier, inc=1, device_id={"space": lax.rem(me + k, NS)}, device_id_type=MESH
+        )
+        return carry
+
+    lax.fori_loop(1, NS, tell, 0)
+    return barrier
+
+
+def send_all(me, out_of, into, send_sem, recv_sem):
+    def start(k, carry):
+        to = lax.rem(me + k, NS)
+        pltpu.make_async_remote_copy(
+            src_ref=out_of(to),
+            dst_ref=into.at[me],
+            send_sem=send_sem.at[to],
+            recv_sem=recv_sem.at[me],
+            device_id={"space": to},
+            device_id_type=MESH,
+        ).start()
+        return carry
+
+    lax.fori_loop(1, NS, start, 0)
+
+
+def wait_all(me, out_of, into, send_sem, recv_sem):
+    def arrive(k, carry):
+        other = lax.rem(me + k, NS)
+        copy = pltpu.make_async_remote_copy(
+            src_ref=out_of(other),
+            dst_ref=into.at[other],
+            send_sem=send_sem.at[other],
+            recv_sem=recv_sem.at[other],
+            device_id={"space": other},
+            device_id_type=MESH,
+        )
+        copy.wait_recv()
+        copy.wait_send()
+        return carry
+
+    lax.fori_loop(1, NS, arrive, 0)
+
+
+def exchange_kernel(
+    orbit_in, props_in, table, cube, next_out, recv_a, recv_b, slot_out,
+    orbit, props, rows, prows, planes, need, needs, send_a, send_b,
+    local_sem, need_send, need_recv, a_send, a_recv, b_send, b_recv,
+):
+    me = lax.axis_index("space")
+    barrier = hello(me)
+    orbit_copy = pltpu.make_async_copy(orbit_in, orbit, local_sem.at[0])
+    props_copy = pltpu.make_async_copy(props_in, props, local_sem.at[1])
+    orbit_copy.start()
+    props_copy.start()
+
+    maps = cube_maps(cube[...])
+    slots = []
+    for to, _ in maps:
+        rank = rank_row(to.astype(F32))
+        slots.append((to.astype(F32) * CAP + rank, jnp.max(rank, axis=1, keepdims=True)))
+    need[...] = jnp.concatenate(
+        [jnp.broadcast_to(most, (1, BLK)) for _, most in slots] + [jnp.zeros((4, BLK), F32)], axis=0
+    )
+    needs[pl.ds(me, 1)] = need[...][None]
+    pl.semaphore_wait(barrier, NS - 1)
+    send_all(me, lambda to: need, needs, need_send, need_recv)
+
+    props_copy.wait()
+    orbit_copy.wait()
+
     def spread(b, carry):
         col = pl.ds(pl.multiple_of(b * BLK, BLK), BLK)
         at = pl.multiple_of(b * 8, 8)
@@ -102,50 +176,31 @@
 
     lax.fori_loop(0, NB, spread, 0, unroll=8)
 
-    tab = jnp.concatenate([table[...], jnp.zeros((1, 64), F32)], axis=1)
-    tab = pltpu.roll(jnp.broadcast_to(tab, (8, BLK)), 1, 1)
-    slope = pltpu.roll(tab, BLK - 1, 1) - tab
-
-    def advance(g, carry):
-        def load(ref, c):
-            return jnp.concatenate(
-                [
-                    ref[pl.ds(g * (chunk * 8) + k * 8 + c, 8, stride=8), :]
-                    for k in range(0, chunk, 8)
-                ],
-                axis=0,
-            )
-
-        at = pl.ds(pl.multiple_of(g * chunk, chunk), chunk)
-        now = tuple(load(rows, c) for c in range(6))
-        drag = load(prows, 2) * (DRAG_SCALE * TIME_STEP)
-        planes[3, at, :] = load(prows, 0)
-        planes[4, at, :] = load(prows, 1)
-        now = lax.fori_loop(0, SUB, lambda s, v: substep(*v, drag, tab, slope), now, unroll=2)
-        for c in range(6):
-            for k in range(0, chunk, 8):
-                rows[pl.ds(g * (chunk * 8) + k * 8 + c, 8, stride=8), :] = now[c][k : k + 8]
-        for c in range(3):
-            planes[c, at, :] = now[3 + c]
-        return carry
-
-    lax.fori_loop(0, NB // chunk, advance, 0)
-
-    def collect(b, carry):
-        col = pl.ds(pl.multiple_of(b * BLK, BLK), BLK)
-        next_out[:, col] = rows[pl.ds(pl.multiple_of(b * 8, 8), 6), :]
-        return carry
-
-    lax.fori_loop(0, NB, collect, 0, unroll=8)
-
-    slot = block_slots(cube[...])
+    def load(ref, c):
+        return jnp.concatenate(
+            [ref[pl.ds(k * 8 + c, 8, stride=8), :] for k in range(0, NB, 8)], axis=0
+        )
+
+    wait_all(me, lambda to: need, needs, need_send, need_recv)
+    worst = jnp.max(needs[...], axis=0)
+    wide = lambda m: jnp.concatenate([worst[m : m + 1]] * 2, axis=1) < CAP
+    slot, local = slots[0][0], maps[0][1]
+    for m in (3, 2, 1):
+        slot = jnp.where(wide(m), slots[m][0], slot)
+        local = jnp.where(wide(m), maps[m][1], local)
+    slot_out[...] = jnp.broadcast_to(slot, (8, NB))
     pick = jnp.where(slot == iota((SLOTS, NB), 0).astype(F32), 1.0, 0.0).astype(BF16)
-    for c in range(5):
-        high, low = split2(planes[c])
+
+    def pack(plane):
+        high, low = split2(plane)
         got = jnp.dot(pick, jnp.concatenate([high, low], axis=1), preferred_element_type=F32)
-        send[:, c * CAP : (c + 1) * CAP, :] = (got[:, :BLK] + got[:, BLK:]).reshape(NS, CAP, BLK)
-    local = ((cube[...] & (CUBES - 1)) + 1).astype(F32)
-    ids = jnp.dot(pick, columns_of(local).astype(BF16), preferred_element_type=F32)
+        return (got[:, :BLK] + got[:, BLK:]).reshape(NS, CAP, BLK)
+
+    send_a[:, :CAP, :] = pack(load(prows, 0))
+    send_a[:, CAP : 2 * CAP, :] = pack(load(prows, 1))
+    ids = jnp.dot(
+        pick, columns_of((local + 1).astype(F32)).astype(BF16), preferred_element_type=F32
+    )
     id_rows = []
     for q in range(SLOTS // BLK):
         line = jnp.transpose(ids[q * BLK : (q + 1) * BLK])[0:1]
@@ -155,7 +210,41 @@
     id_rows = jnp.where(mine, id_rows, 0.0)
     id_rows = id_rows + pltpu.roll(id_rows, 64, 1)
     id_rows = id_rows + pltpu.roll(id_rows, 32, 1)
-    send[:, 5 * CAP :, :] = jnp.broadcast_to(id_rows[:, None, :], (NS, 8, BLK))
+    send_a[:, 2 * CAP :, :] = jnp.broadcast_to(id_rows[:, None, :], (NS, 8, BLK))
+    keep_a = pltpu.make_async_copy(send_a.at[me], recv_a.at[me], local_sem.at[2])
+    keep_a.start()
+    send_all(me, lambda to: send_a.at[to], recv_a, a_send, a_recv)
+
+    tab = jnp.concatenate([table[...], jnp.zeros((1, 64), F32)], axis=1)
+    tab = pltpu.roll(jnp.broadcast_to(tab, (8, BLK)), 1, 1)
+    slope = pltpu.roll(tab, BLK - 1, 1) - tab
+    now = tuple(load(rows, c) for c in range(6))
+    drag = load(prows, 2) * (DRAG_SCALE * TIME_STEP)
+    now = lax.fori_loop(0, SUB, lambda s, v: substep(*v, drag, tab, slope), now, unroll=2)
+    for c in range(6):
+        for k in range(0, NB, 8):
+            rows[pl.ds(k * 8 + c, 8, stride=8), :] = now[c][k : k + 8]
+    for c in range(3):
+        planes[c] = now[3 + c]
+    for c in range(3):
+        send_b[:, c * CAP : (c + 1) * CAP, :] = pack(planes[c])
+    keep_b = pltpu.make_async_copy(send_b.at[me], recv_b.at[me], local_sem.at[3])
+    keep_b.start()
+    send_all(me, lambda to: send_b.at[to], recv_b, b_send, b_recv)
+
+    def collect(b, carry):
+        col = pl.ds(pl.multiple_of(b * BLK, BLK), BLK)
+        orbit[:, col] = rows[pl.ds(pl.multiple_of(b * 8, 8), 6), :]
+        return carry
+
+    lax.fori_loop(0, NB, collect, 0, unroll=8)
+    next_copy = pltpu.make_async_copy(orbit, next_out, local_sem.at[0])
+    next_copy.start()
+    keep_a.wait()
+    keep_b.wait()
+    wait_all(me, lambda to: send_a.at[to], recv_a, a_send, a_recv)
+    wait_all(me, lambda to: send_b.at[to], recv_b, b_send, b_recv)
+    next_copy.wait()
 
 
 def features(planes):
@@ -188,18 +277,42 @@
     return left, right
 
 
-def pair_kernel(recv, back, left, right, rate):
-    got = recv[:, 5 * CAP, :]
+def cube_order(ids):
+    column = columns_of(ids)
+    ranks, counts = [], []
+    for k in range(0, SLOTS, BLK):
+        same = column == ids[:, k : k + BLK]
+        earlier = iota((SLOTS, BLK), 0) < iota((SLOTS, BLK), 1) + k
+        ranks.append(jnp.sum(jnp.where(earlier & same, 1.0, 0.0), axis=0, keepdims=True))
+        counts.append(jnp.sum(jnp.where(same, 1.0, 0.0), axis=0, keepdims=True))
+    rank, count = jnp.concatenate(ranks, axis=1), jnp.concatenate(counts, axis=1)
+    key = (MOST - count) * 256.0 + ids
+    first = (ids > 0.0) & (rank == 0.0)
+    first_keys = columns_of(jnp.where(first, key, 1e9))
+    before = [
+        jnp.sum(jnp.where(first_keys < key[:, k : k + BLK], 1.0, 0.0), axis=0, keepdims=True)
+        for k in range(0, SLOTS, BLK)
+    ]
+    place = jnp.where(ids > 0.0, jnp.concatenate(before, axis=1) * MOST + rank, -1.0)
+    cubes = [
+        jnp.sum(jnp.where(first & (count >= n), 1.0, 0.0)).astype(jnp.int32)
+        for n in range(MOST, 0, -1)
+    ]
+    return place, cubes
+
+
+def pair_kernel(recv_a, recv_b, back, left, right, rate):
+    got = recv_a[:, 2 * CAP, :]
     mine = lax.shift_right_logical(iota((NS, BLK), 1), 5) == (iota((NS, BLK), 0) & 3)
     got = jnp.where(mine, got, 0.0)
     ids = jnp.concatenate(
         [jnp.sum(got[4 * q : 4 * q + 4], axis=0, keepdims=True) for q in range(4)], axis=1
     )
-    place = jnp.where(ids > 0.0, (ids - 1.0) * MOST + rank_row(ids), -1.0)
+    place, cubes = cube_order(ids)
     pick = jnp.where(place == iota((SLOTS, SLOTS), 0).astype(F32), 1.0, 0.0).astype(BF16)
     planes = []
-    for c in range(5):
-        plane = recv[:, c * CAP : (c + 1) * CAP, :].reshape(SLOTS, BLK)
+    for ref, c in ((recv_b, 0), (recv_b, 1), (recv_b, 2), (recv_a, 0), (recv_a, 1)):
+        plane = ref[:, c * CAP : (c + 1) * CAP, :].reshape(SLOTS, BLK)
         high, low = split2(plane)
         out = jnp.dot(pick, jnp.concatenate([high, low], axis=1), preferred_element_type=F32)
         planes.append((out[:, :BLK], out[:, BLK:]))
@@ -212,14 +325,16 @@
     gap_rows = iota((KF, BLK), 0) < 18
     off_diag = iota((BLK, BLK), 0) != iota((BLK, BLK), 1)
 
-    def one_cube(q):
+    rate[...] = zero
+
+    def one_cube(q, members):
         base = q * MOST
         lhs = jnp.concatenate(
-            [left[pl.ds(base + m, KF, stride=PITCH), :].astype(BF16) for m in range(MOST)], axis=1
+            [left[pl.ds(base + m, KF, stride=PITCH), :].astype(BF16) for m in range(members)], axis=1
         )
-        row_sums = [None] * MOST
+        row_sums = [None] * members
         out = []
-        for c in range(MOST):
+        for c in range(members):
             r = right[pl.ds(base + c, KF, stride=PITCH), :]
             rhs = jnp.concatenate(
                 [jnp.where(gap_rows, r, 0.0), jnp.where(gap_rows, 0.0, r)], axis=1
@@ -238,17 +353,23 @@
                 part = jnp.sum(pair.reshape(16, 8, BLK), axis=0)
                 total = part if total is None else total + part
             out.append(total)
-        for c in range(MOST):
+        for c in range(members):
             total = out[c]
             if row_sums[c] is not None:
                 total = total + jnp.sum(jnp.transpose(row_sums[c]).reshape(16, 8, BLK), axis=0)
             rate[pl.ds(base + c, 1), :] = jnp.sum(total, axis=0, keepdims=True) * (1.0 / (MOST * BLK))
 
-    def cubes(q, carry):
-        one_cube(q)
-        return carry
-
-    lax.fori_loop(0, CUBES, cubes, 0, unroll=8)
+    done = 0
+    for members, ahead in zip(range(MOST, 0, -1), cubes):
+        upto = lax.div(ahead + (GROUP - 1), GROUP)
+
+        def group(g, carry, members=members):
+            for k in range(GROUP):
+                one_cube(g * GROUP + k, members)
+            return carry
+
+        lax.fori_loop(done, upto, group, 0)
+        done = upto
 
     place_col = columns_of(place)
     unpick = jnp.concatenate(
@@ -263,8 +384,10 @@
     back[...] = (out[:, :BLK] + out[:, BLK:]).reshape(NS, CAP, BLK)
 
 
-def unpack_kernel(back, cube, out):
-    slot_col = columns_of(block_slots(cube[...]))
+def return_kernel(back, slot, out, home, kept_sem, send_sem, recv_sem):
+    me = lax.axis_index("space")
+    barrier = hello(me)
+    slot_col = columns_of(slot[0:1, :])
     pick = jnp.concatenate(
         [
             jnp.where(slot_col == (iota((NB, BLK), 1) + k).astype(F32), 1.0, 0.0)
@@ -272,69 +395,91 @@
         ],
         axis=1,
     ).astype(BF16)
-    high, low = split2(back[...].reshape(SLOTS, BLK))
+    kept = pltpu.make_async_copy(back.at[me], home.at[me], kept_sem)
+    kept.start()
+    pl.semaphore_wait(barrier, NS - 1)
+    send_all(me, lambda to: back.at[to], home, send_sem, recv_sem)
+    kept.wait()
+    wait_all(me, lambda to: back.at[to], home, send_sem, recv_sem)
+    high, low = split2(home[...].reshape(SLOTS, BLK))
     got = jnp.dot(pick, jnp.concatenate([high, low], axis=1), preferred_element_type=F32)
     out[...] = got[:, :BLK] + got[:, BLK:]
 
 
 VMEM = pl.BlockSpec(memory_space=pltpu.VMEM)
-PARAMS = pltpu.CompilerParams(vmem_limit_bytes=56 * 2**20)
-
-
-def propagate_call(orbit_state, object_props, table, cube, chunk=256):
+ANY = pl.BlockSpec(memory_space=pl.ANY)
+LIMIT = 56 * 2**20
+DMA = pltpu.SemaphoreType.DMA
+
+
+def exchange_call(orbit_state, object_props, table, cube):
+    many = NB * BLK
     return pl.pallas_call(
-        functools.partial(propagate_kernel, chunk),
+        exchange_kernel,
         out_shape=(
-            jax.ShapeDtypeStruct((6, NB * BLK), F32),
-            jax.ShapeDtypeStruct((NS, ROWS, BLK), F32),
+            jax.ShapeDtypeStruct((6, many), F32),
+            jax.ShapeDtypeStruct((NS, 2 * CAP + 8, BLK), F32),
+            jax.ShapeDtypeStruct((NS, 3 * CAP, BLK), F32),
+            jax.ShapeDtypeStruct((8, NB), F32),
         ),
-        in_specs=[VMEM] * 4,
-        out_specs=(VMEM, VMEM),
+        in_specs=[ANY, ANY, VMEM, VMEM],
+        out_specs=(ANY, ANY, ANY, VMEM),
         scratch_shapes=[
+            pltpu.VMEM((6, many), F32),
+            pltpu.VMEM((3, many), F32),
             pltpu.VMEM((NB * 8, BLK), F32),
             pltpu.VMEM((NB * 8, BLK), F32),
+            pltpu.VMEM((3, NB, BLK), F32),
             pltpu.VMEM((8, BLK), F32),
-            pltpu.VMEM((5, NB, BLK), F32),
-        ],
-        compiler_params=PARAMS,
-        name="propagate",
+            pltpu.VMEM((NS, 8, BLK), F32),
+            pltpu.VMEM((NS, 2 * CAP + 8, BLK), F32),
+            pltpu.VMEM((NS, 3 * CAP, BLK), F32),
+            DMA((4,)),
+        ]
+        + [DMA((NS,))] * 6,
+        compiler_params=pltpu.CompilerParams(
+            collective_id=0, has_side_effects=True, vmem_limit_bytes=LIMIT
+        ),
+        name="exchange",
     )(orbit_state, object_props, table, cube)
 
 
-def pair_call(recv):
+def pair_call(recv_a, recv_b):
     return pl.pallas_call(
         pair_kernel,
         out_shape=jax.ShapeDtypeStruct((NS, CAP, BLK), F32),
-        in_specs=[VMEM],
+        in_specs=[VMEM, VMEM],
         out_specs=VMEM,
         scratch_shapes=[
             pltpu.VMEM((KF * PITCH, BLK), F32),
             pltpu.VMEM((KF * PITCH, BLK), F32),
             pltpu.VMEM((SLOTS, BLK), F32),
         ],
-        compiler_params=PARAMS,
+        compiler_params=pltpu.CompilerParams(vmem_limit_bytes=LIMIT),
         name="pairs",
-    )(recv)
-
-
-def unpack_call(back, cube):
+    )(recv_a, recv_b)
+
+
+def return_call(back, slot):
     return pl.pallas_call(
-        unpack_kernel,
+        return_kernel,
         out_shape=jax.ShapeDtypeStruct((NB, BLK), F32),
-        in_specs=[VMEM] * 2,
+        in_specs=[VMEM, VMEM],
         out_specs=VMEM,
-        compiler_params=PARAMS,
-        name="unpack",
-    )(back, cube)
+        scratch_shapes=[pltpu.VMEM((NS, CAP, BLK), F32), DMA, DMA((NS,)), DMA((NS,))],
+        compiler_params=pltpu.CompilerParams(
+            collective_id=1, has_side_effects=True, vmem_limit_bytes=LIMIT
+        ),
+        name="bring_home",
+    )(back, slot)
 
 
 def on_device(orbit_state, object_props, density_table, block_cube):
-    cube = block_cube.reshape(1, NB)
-    next_state, send = propagate_call(orbit_state, object_props, density_table.reshape(1, 64), cube)
-    recv = lax.all_to_all(send, "space", split_axis=0, concat_axis=0, tiled=True)
-    back = pair_call(recv)
-    home = lax.all_to_all(back, "space", split_axis=0, concat_axis=0, tiled=True)
-    return next_state, unpack_call(home, cube).reshape(NB * BLK)
+    next_state, recv_a, recv_b, slot = exchange_call(
+        orbit_state, object_props, density_table.reshape(1, 64), block_cube.reshape(1, NB)
+    )
+    back = pair_call(recv_a, recv_b)
+    return next_state, return_call(back, slot).reshape(NB * BLK)
 
 
 def solution(mesh):

time: 85.4 us -> 62.2 us (0.73)
  blocking collectives: 40.3 us -> 0 us
  Pallas kernels: 44.1 us -> 59.3 us
  local copies, waits for them, and re-layouts: 0 us -> 1.66 us
    all_to_all x2 -> x0, blocking collectives: 40.3 us -> none  [the longest x1 27.6 us: on_device(): lax.all_to_all(send, 'space', split_axis=0, concat_axis=0, tiled=True)]
    pallas_call x2, Pallas kernels: 13.2 us -> 43.1 us  [the longest x1 30.8 us: exchange_call(): pl.pallas_call(exchange_kernel, out_shape=(jax.ShapeDtypeStruct((6, many)...]
    pallas_call x1, Pallas kernels: 30.9 us -> 16.2 us  [pair_call(): pl.pallas_call(pair_kernel, out_shape=jax.ShapeDtypeStruct((NS, CAP, BLK)...]
    unnamed x0 -> x6, local copies, waits for them, and re-layouts: none -> 1.66 us
where the time goes in v3:
time: 62.2 us; the launch traced here: 61.6 us
  Pallas kernels  59.3 us (95%)
  local copies, waits for them, and re-layouts  1.66 us (3%)
  between operations  0.67 us (1%)
    pallas_call x1, Pallas kernels, exchange_call(): pl.pallas_call(exchange_kernel, out_shape=(jax.ShapeDtypeStruct((6, many)...  30.8 us
    pallas_call x1, Pallas kernels, pair_call(): pl.pallas_call(pair_kernel, out_shape=jax.ShapeDtypeStruct((NS, CAP, BLK)...  16.2 us
    pallas_call x1, Pallas kernels, return_call(): pl.pallas_call(return_kernel, out_shape=jax.ShapeDtypeStruct((NB, BLK), F...  12.3 us
    unnamed x6, local copies, waits for them, and re-layouts  1.66 us

profile of v3, /device:TPU:0, one launch (start us, length us, event | category | flops | bytes accessed | tf_op | source)
XLA Modules:
  0.0 61.6 jit_solution(8343593070428450716)
XLA Ops:
  0.6 30.8 %exchange.1 = (f32[6,32768]{1,0:T(8,128)}, f32[16,72,128]{2,1,0:T(8,128)}, f32[16,96,128]{2,1,0:T(8,128)}, f32[8,256]{1,0:T(8,128)}) custom-call(f32[6,32768]{1,0:T(8,128)} %orbit_in.1, f32[3,32768]{1,0:T(4,128)} %props_in.1, f32[1,64]{1,0:T(1,128)} %bitcast.5, s32[1,256]{1,0:T(1,128)} %bitcast.4), custom_call_target="tpu_custom_call" | custom-call | tf_op jit(solution)/shard_map/exchange/pallas_call | solution.py:417
  31.4 0.0 copy-start
  31.4 16.2 %pairs.1.back = f32[16,32,128]{2,1,0:T(8,128)} custom-call(f32[16,72,128]{2,1,0:T(8,128)} %get-tuple-element.7.recv_a, f32[16,96,128]{2,1,0:T(8,128)} %get-tuple-element.8.recv_b), custom_call_target="tpu_custom_call" | custom-call | tf_op jit(solution)/shard_map/pairs/pallas_call | solution.py:448
  47.6 12.3 %bring_home.1 = f32[256,128]{1,0:T(8,128)} custom-call(f32[16,32,128]{2,1,0:T(8,128)} %pairs.1.back, f32[8,256]{1,0:T(8,128)} %get-tuple-element.9.slot), custom_call_target="tpu_custom_call" | custom-call | tf_op jit(solution)/shard_map/bring_home/pallas_call | solution.py:464
  60.0 0.0 copy-done
  60.0 0.0 copy-start.1
  60.0 1.0 %copy.8 = f32[6,32768]{1,0:T(8,128)} copy(f32[6,32768]{1,0:T(8,128)S(1)} %copy-done) | data formatting | bytes 1572864
  61.0 0.0 copy-done.1
  61.0 0.7 %copy.9 = f32[32768]{0:T(1024)} copy(f32[32768]{0:T(1024)S(1)} %bitcast.3) | data formatting | bytes 262144
Async XLA Ops:
  31.4 28.6 %copy-start = (f32[6,32768]{1,0:T(8,128)S(1)}, f32[6,32768]{1,0:T(8,128)}, u32[]{:S(2)}) copy-start(f32[6,32768]{1,0:T(8,128)} %get-tuple-element.12) | copy-start | bytes 2359300
  60.0 1.0 %copy-start.1 = (f32[256,128]{1,0:T(8,128)S(1)}, f32[256,128]{1,0:T(8,128)}, u32[]{:S(2)}) copy-start(f32[256,128]{1,0:T(8,128)} %bring_home.1) | copy-start | bytes 393220

commit v4 on v3

--- a/solution.py
+++ b/solution.py
@@ -140,30 +140,50 @@
     lax.fori_loop(1, NS, arrive, 0)
 
 
+def one_hot(place, n):
+    width = place.shape[1]
+    return jnp.where(place == iota((n, width), 0).astype(F32), 1.0, 0.0).astype(BF16)
+
+
+def one_hot_back(place):
+    column = columns_of(place)
+    n = place.shape[1]
+    parts = [
+        jnp.where(column == (iota((n, BLK), 1) + k).astype(F32), 1.0, 0.0)
+        for k in range(0, SLOTS, BLK)
+    ]
+    return jnp.concatenate(parts, axis=1).astype(BF16)
+
+
+def picked(pick, plane):
+    high, low = split2(plane)
+    got = jnp.dot(pick, jnp.concatenate([high, low], axis=1), preferred_element_type=F32)
+    return got[:, :BLK] + got[:, BLK:]
+
+
 def exchange_kernel(
-    orbit_in, props_in, table, cube, next_out, recv_a, recv_b, slot_out,
-    orbit, props, rows, prows, planes, need, needs, send_a, send_b,
-    local_sem, need_send, need_recv, a_send, a_recv, b_send, b_recv,
+    orbit_in, props_in, table, cube, next_out, grouped_out, place_out, count_out, slot_out,
+    orbit, props, rows, prows, need, needs, send_a, send_b, recv_a, recv_b, grouped,
+    local_sem, group_sem, need_send, need_recv, a_send, a_recv, b_send, b_recv,
 ):
     me = lax.axis_index("space")
     barrier = hello(me)
     orbit_copy = pltpu.make_async_copy(orbit_in, orbit, local_sem.at[0])
     props_copy = pltpu.make_async_copy(props_in, props, local_sem.at[1])
+    props_copy.start()
     orbit_copy.start()
-    props_copy.start()
 
     maps = cube_maps(cube[...])
-    slots = []
+    most = []
     for to, _ in maps:
-        rank = rank_row(to.astype(F32))
-        slots.append((to.astype(F32) * CAP + rank, jnp.max(rank, axis=1, keepdims=True)))
-    need[...] = jnp.concatenate(
-        [jnp.broadcast_to(most, (1, BLK)) for _, most in slots] + [jnp.zeros((4, BLK), F32)], axis=0
-    )
+        held = jnp.sum(jnp.where(to == iota((NS, NB), 0), 1.0, 0.0), axis=1, keepdims=True)
+        most.append(jnp.broadcast_to(jnp.max(held, axis=0, keepdims=True), (1, BLK)))
+    need[...] = jnp.concatenate(most + [jnp.zeros((4, BLK), F32)], axis=0)
     needs[pl.ds(me, 1)] = need[...][None]
     pl.semaphore_wait(barrier, NS - 1)
     send_all(me, lambda to: need, needs, need_send, need_recv)
 
+    slots = [to.astype(F32) * CAP + rank_row(to.astype(F32)) for to, _ in maps]
     props_copy.wait()
     orbit_copy.wait()
 
@@ -183,21 +203,15 @@
 
     wait_all(me, lambda to: need, needs, need_send, need_recv)
     worst = jnp.max(needs[...], axis=0)
-    wide = lambda m: jnp.concatenate([worst[m : m + 1]] * 2, axis=1) < CAP
-    slot, local = slots[0][0], maps[0][1]
+    wide = lambda m: jnp.concatenate([worst[m : m + 1]] * 2, axis=1) <= CAP
+    slot, local = slots[0], maps[0][1]
     for m in (3, 2, 1):
-        slot = jnp.where(wide(m), slots[m][0], slot)
+        slot = jnp.where(wide(m), slots[m], slot)
         local = jnp.where(wide(m), maps[m][1], local)
     slot_out[...] = jnp.broadcast_to(slot, (8, NB))
-    pick = jnp.where(slot == iota((SLOTS, NB), 0).astype(F32), 1.0, 0.0).astype(BF16)
-
-    def pack(plane):
-        high, low = split2(plane)
-        got = jnp.dot(pick, jnp.concatenate([high, low], axis=1), preferred_element_type=F32)
-        return (got[:, :BLK] + got[:, BLK:]).reshape(NS, CAP, BLK)
-
-    send_a[:, :CAP, :] = pack(load(prows, 0))
-    send_a[:, CAP : 2 * CAP, :] = pack(load(prows, 1))
+    pick = one_hot(slot, SLOTS)
+    send_a[:, :CAP, :] = picked(pick, load(prows, 0)).reshape(NS, CAP, BLK)
+    send_a[:, CAP : 2 * CAP, :] = picked(pick, load(prows, 1)).reshape(NS, CAP, BLK)
     ids = jnp.dot(
         pick, columns_of((local + 1).astype(F32)).astype(BF16), preferred_element_type=F32
     )
@@ -211,9 +225,8 @@
     id_rows = id_rows + pltpu.roll(id_rows, 64, 1)
     id_rows = id_rows + pltpu.roll(id_rows, 32, 1)
     send_a[:, 2 * CAP :, :] = jnp.broadcast_to(id_rows[:, None, :], (NS, 8, BLK))
-    keep_a = pltpu.make_async_copy(send_a.at[me], recv_a.at[me], local_sem.at[2])
-    keep_a.start()
     send_all(me, lambda to: send_a.at[to], recv_a, a_send, a_recv)
+    recv_a[pl.ds(me, 1)] = send_a[pl.ds(me, 1)]
 
     tab = jnp.concatenate([table[...], jnp.zeros((1, 64), F32)], axis=1)
     tab = pltpu.roll(jnp.broadcast_to(tab, (8, BLK)), 1, 1)
@@ -225,12 +238,8 @@
         for k in range(0, NB, 8):
             rows[pl.ds(k * 8 + c, 8, stride=8), :] = now[c][k : k + 8]
     for c in range(3):
-        planes[c] = now[3 + c]
-    for c in range(3):
-        send_b[:, c * CAP : (c + 1) * CAP, :] = pack(planes[c])
-    keep_b = pltpu.make_async_copy(send_b.at[me], recv_b.at[me], local_sem.at[3])
-    keep_b.start()
-    send_all(me, lambda to: send_b.at[to], recv_b, b_send, b_recv)
+        send_b[c] = picked(pick, load(rows, 3 + c)).reshape(NS, CAP, BLK)
+        send_all(me, lambda to: send_b.at[c, to], recv_b.at[c], b_send.at[c], b_recv.at[c])
 
     def collect(b, carry):
         col = pl.ds(pl.multiple_of(b * BLK, BLK), BLK)
@@ -240,18 +249,44 @@
     lax.fori_loop(0, NB, collect, 0, unroll=8)
     next_copy = pltpu.make_async_copy(orbit, next_out, local_sem.at[0])
     next_copy.start()
-    keep_a.wait()
-    keep_b.wait()
+    for c in range(3):
+        recv_b[c, pl.ds(me, 1)] = send_b[c, pl.ds(me, 1)]
+
     wait_all(me, lambda to: send_a.at[to], recv_a, a_send, a_recv)
-    wait_all(me, lambda to: send_b.at[to], recv_b, b_send, b_recv)
+    got = jnp.where(mine, recv_a[:, 2 * CAP, :], 0.0)
+    ids = jnp.concatenate(
+        [jnp.sum(got[4 * q : 4 * q + 4], axis=0, keepdims=True) for q in range(4)], axis=1
+    )
+    place, counts = cube_order(ids)
+    place_out[...] = jnp.broadcast_to(place, (8, SLOTS))
+    count_out[...] = counts
+    pick = one_hot(place, SLOTS)
+
+    def regroup(c, plane):
+        grouped[c] = picked(pick, plane.reshape(SLOTS, BLK))
+        copy = pltpu.make_async_copy(grouped.at[c], grouped_out.at[c], group_sem.at[c])
+        copy.start()
+        return copy
+
+    copies = [
+        regroup(3, recv_a[:, :CAP, :]),
+        regroup(4, recv_a[:, CAP : 2 * CAP, :]),
+    ]
+    for c in range(3):
+        wait_all(me, lambda to: send_b.at[c, to], recv_b.at[c], b_send.at[c], b_recv.at[c])
+        copies.append(regroup(c, recv_b[c]))
+    for copy in copies:
+        copy.wait()
     next_copy.wait()
 
 
 def features(planes):
-    v, (rh, rm), (wh, wm) = planes[:3], planes[3], planes[4]
-    radius, weight = rh + rm, wh + wm
-    full = [h + m for h, m in v]
-    norm = full[0] * full[0] + full[1] * full[1] + full[2] * full[2]
+    radius, weight = planes[3], planes[4]
+    v = []
+    for full in planes[:3]:
+        high = full.astype(BF16).astype(F32)
+        v.append((high, full - high))
+    norm = planes[0] * planes[0] + planes[1] * planes[1] + planes[2] * planes[2]
 
     def thirds(x):
         a = x.astype(BF16).astype(F32)
@@ -295,28 +330,18 @@
     ]
     place = jnp.where(ids > 0.0, jnp.concatenate(before, axis=1) * MOST + rank, -1.0)
     cubes = [
-        jnp.sum(jnp.where(first & (count >= n), 1.0, 0.0)).astype(jnp.int32)
+        jnp.broadcast_to(
+            jnp.sum(jnp.where(first & (count >= n), 1, 0), axis=1, keepdims=True), (1, BLK)
+        )
         for n in range(MOST, 0, -1)
     ]
-    return place, cubes
-
-
-def pair_kernel(recv_a, recv_b, back, left, right, rate):
-    got = recv_a[:, 2 * CAP, :]
-    mine = lax.shift_right_logical(iota((NS, BLK), 1), 5) == (iota((NS, BLK), 0) & 3)
-    got = jnp.where(mine, got, 0.0)
-    ids = jnp.concatenate(
-        [jnp.sum(got[4 * q : 4 * q + 4], axis=0, keepdims=True) for q in range(4)], axis=1
-    )
-    place, cubes = cube_order(ids)
-    pick = jnp.where(place == iota((SLOTS, SLOTS), 0).astype(F32), 1.0, 0.0).astype(BF16)
-    planes = []
-    for ref, c in ((recv_b, 0), (recv_b, 1), (recv_b, 2), (recv_a, 0), (recv_a, 1)):
-        plane = ref[:, c * CAP : (c + 1) * CAP, :].reshape(SLOTS, BLK)
-        high, low = split2(plane)
-        out = jnp.dot(pick, jnp.concatenate([high, low], axis=1), preferred_element_type=F32)
-        planes.append((out[:, :BLK], out[:, BLK:]))
-    lefts, rights = features(planes)
+    return place, jnp.concatenate(cubes + [jnp.zeros((4, BLK), jnp.int32)], axis=0)
+
+
+def pair_kernel(next_in, grouped, counts, next_out, rate, left, right, sem):
+    next_copy = pltpu.make_async_copy(next_in, next_out, sem)
+    next_copy.start()
+    lefts, rights = features([grouped[c] for c in range(5)])
     zero = jnp.zeros((SLOTS, BLK), F32)
     for f in range(KF):
         left[f * PITCH : f * PITCH + SLOTS, :] = lefts[f] if f < len(lefts) else zero
@@ -360,8 +385,8 @@
             rate[pl.ds(base + c, 1), :] = jnp.sum(total, axis=0, keepdims=True) * (1.0 / (MOST * BLK))
 
     done = 0
-    for members, ahead in zip(range(MOST, 0, -1), cubes):
-        upto = lax.div(ahead + (GROUP - 1), GROUP)
+    for row, members in enumerate(range(MOST, 0, -1)):
+        upto = lax.div(counts[row, 0] + (GROUP - 1), GROUP)
 
         def group(g, carry, members=members):
             for k in range(GROUP):
@@ -371,39 +396,19 @@
         lax.fori_loop(done, upto, group, 0)
         done = upto
 
-    place_col = columns_of(place)
-    unpick = jnp.concatenate(
-        [
-            jnp.where(place_col == (iota((SLOTS, BLK), 1) + k).astype(F32), 1.0, 0.0)
-            for k in range(0, SLOTS, BLK)
-        ],
-        axis=1,
-    ).astype(BF16)
-    high, low = split2(rate[...])
-    out = jnp.dot(unpick, jnp.concatenate([high, low], axis=1), preferred_element_type=F32)
-    back[...] = (out[:, :BLK] + out[:, BLK:]).reshape(NS, CAP, BLK)
-
-
-def return_kernel(back, slot, out, home, kept_sem, send_sem, recv_sem):
+    next_copy.wait()
+
+
+def return_kernel(rate, place, slot, out, back, home, send_sem, recv_sem):
     me = lax.axis_index("space")
     barrier = hello(me)
-    slot_col = columns_of(slot[0:1, :])
-    pick = jnp.concatenate(
-        [
-            jnp.where(slot_col == (iota((NB, BLK), 1) + k).astype(F32), 1.0, 0.0)
-            for k in range(0, SLOTS, BLK)
-        ],
-        axis=1,
-    ).astype(BF16)
-    kept = pltpu.make_async_copy(back.at[me], home.at[me], kept_sem)
-    kept.start()
+    back[...] = picked(one_hot_back(place[0:1, :]), rate[...]).reshape(NS, CAP, BLK)
+    home[pl.ds(me, 1)] = back[pl.ds(me, 1)]
     pl.semaphore_wait(barrier, NS - 1)
     send_all(me, lambda to: back.at[to], home, send_sem, recv_sem)
-    kept.wait()
+    pick = one_hot_back(slot[0:1, :])
     wait_all(me, lambda to: back.at[to], home, send_sem, recv_sem)
-    high, low = split2(home[...].reshape(SLOTS, BLK))
-    got = jnp.dot(pick, jnp.concatenate([high, low], axis=1), preferred_element_type=F32)
-    out[...] = got[:, :BLK] + got[:, BLK:]
+    out[...] = picked(pick, home[...].reshape(SLOTS, BLK))
 
 
 VMEM = pl.BlockSpec(memory_space=pltpu.VMEM)
@@ -418,25 +423,34 @@
         exchange_kernel,
         out_shape=(
             jax.ShapeDtypeStruct((6, many), F32),
-            jax.ShapeDtypeStruct((NS, 2 * CAP + 8, BLK), F32),
-            jax.ShapeDtypeStruct((NS, 3 * CAP, BLK), F32),
+            jax.ShapeDtypeStruct((5, SLOTS, BLK), F32),
+            jax.ShapeDtypeStruct((8, SLOTS), F32),
+            jax.ShapeDtypeStruct((8, BLK), jnp.int32),
             jax.ShapeDtypeStruct((8, NB), F32),
         ),
         in_specs=[ANY, ANY, VMEM, VMEM],
-        out_specs=(ANY, ANY, ANY, VMEM),
+        out_specs=(ANY, ANY, VMEM, VMEM, VMEM),
         scratch_shapes=[
             pltpu.VMEM((6, many), F32),
             pltpu.VMEM((3, many), F32),
             pltpu.VMEM((NB * 8, BLK), F32),
             pltpu.VMEM((NB * 8, BLK), F32),
-            pltpu.VMEM((3, NB, BLK), F32),
             pltpu.VMEM((8, BLK), F32),
             pltpu.VMEM((NS, 8, BLK), F32),
             pltpu.VMEM((NS, 2 * CAP + 8, BLK), F32),
-            pltpu.VMEM((NS, 3 * CAP, BLK), F32),
-            DMA((4,)),
-        ]
-        + [DMA((NS,))] * 6,
+            pltpu.VMEM((3, NS, CAP, BLK), F32),
+            pltpu.VMEM((NS, 2 * CAP + 8, BLK), F32),
+            pltpu.VMEM((3, NS, CAP, BLK), F32),
+            pltpu.VMEM((5, SLOTS, BLK), F32),
+            DMA((2,)),
+            DMA((5,)),
+            DMA((NS,)),
+            DMA((NS,)),
+            DMA((NS,)),
+            DMA((NS,)),
+            DMA((3, NS)),
+            DMA((3, NS)),
+        ],
         compiler_params=pltpu.CompilerParams(
             collective_id=0, has_side_effects=True, vmem_limit_bytes=LIMIT
         ),
@@ -444,42 +458,50 @@
     )(orbit_state, object_props, table, cube)
 
 
-def pair_call(recv_a, recv_b):
+def pair_call(next_state, grouped, counts):
     return pl.pallas_call(
         pair_kernel,
-        out_shape=jax.ShapeDtypeStruct((NS, CAP, BLK), F32),
-        in_specs=[VMEM, VMEM],
-        out_specs=VMEM,
+        out_shape=(
+            jax.ShapeDtypeStruct(next_state.shape, F32),
+            jax.ShapeDtypeStruct((SLOTS, BLK), F32),
+        ),
+        in_specs=[ANY, VMEM, pl.BlockSpec(memory_space=pltpu.SMEM)],
+        out_specs=(ANY, VMEM),
         scratch_shapes=[
             pltpu.VMEM((KF * PITCH, BLK), F32),
             pltpu.VMEM((KF * PITCH, BLK), F32),
-            pltpu.VMEM((SLOTS, BLK), F32),
+            DMA,
         ],
         compiler_params=pltpu.CompilerParams(vmem_limit_bytes=LIMIT),
         name="pairs",
-    )(recv_a, recv_b)
-
-
-def return_call(back, slot):
+    )(next_state, grouped, counts)
+
+
+def return_call(rate, place, slot):
     return pl.pallas_call(
         return_kernel,
         out_shape=jax.ShapeDtypeStruct((NB, BLK), F32),
-        in_specs=[VMEM, VMEM],
+        in_specs=[VMEM, VMEM, VMEM],
         out_specs=VMEM,
-        scratch_shapes=[pltpu.VMEM((NS, CAP, BLK), F32), DMA, DMA((NS,)), DMA((NS,))],
+        scratch_shapes=[
+            pltpu.VMEM((NS, CAP, BLK), F32),
+            pltpu.VMEM((NS, CAP, BLK), F32),
+            DMA((NS,)),
+            DMA((NS,)),
+        ],
         compiler_params=pltpu.CompilerParams(
             collective_id=1, has_side_effects=True, vmem_limit_bytes=LIMIT
         ),
         name="bring_home",
-    )(back, slot)
+    )(rate, place, slot)
 
 
 def on_device(orbit_state, object_props, density_table, block_cube):
-    next_state, recv_a, recv_b, slot = exchange_call(
+    moved, grouped, place, counts, slot = exchange_call(
         orbit_state, object_props, density_table.reshape(1, 64), block_cube.reshape(1, NB)
     )
-    back = pair_call(recv_a, recv_b)
-    return next_state, return_call(back, slot).reshape(NB * BLK)
+    next_state, rate = pair_call(moved, grouped, counts)
+    return next_state, return_call(rate, place, slot).reshape(NB * BLK)
 
 
 def solution(mesh):

time: 62.2 us -> 80.9 us (1.30)
  Pallas kernels: 59.3 us -> 78.5 us
    pallas_call x1, Pallas kernels: 16.2 us -> 34.9 us  [pair_call(): pl.pallas_call(pair_kernel, out_shape=(jax.ShapeDtypeStruct(next_state.sh...]
    pallas_call x1, Pallas kernels: 30.8 us -> 32.8 us  [exchange_call(): pl.pallas_call(exchange_kernel, out_shape=(jax.ShapeDtypeStruct((6, many)...]
    pallas_call x1, Pallas kernels: 12.3 us -> 10.8 us  [return_call(): pl.pallas_call(return_kernel, out_shape=jax.ShapeDtypeStruct((NB, BLK), F...]
    unnamed x6 -> x1, local copies, waits for them, and re-layouts: 1.66 us -> 1.57 us
where the time goes in v4:
time: 80.9 us; the launch traced here: 80.7 us
  Pallas kernels  78.5 us (97%)
  local copies, waits for them, and re-layouts  1.57 us (2%)
    pallas_call x1, Pallas kernels, pair_call(): pl.pallas_call(pair_kernel, out_shape=(jax.ShapeDtypeStruct(next_state.sh...  34.9 us
    pallas_call x1, Pallas kernels, exchange_call(): pl.pallas_call(exchange_kernel, out_shape=(jax.ShapeDtypeStruct((6, many)...  32.8 us
    pallas_call x1, Pallas kernels, return_call(): pl.pallas_call(return_kernel, out_shape=jax.ShapeDtypeStruct((NB, BLK), F...  10.8 us

profile of v4, /device:TPU:0, one launch (start us, length us, event | category | flops | bytes accessed | tf_op | source)
XLA Modules:
  0.0 80.7 jit_solution(10220233689758811985)
XLA Ops:
  0.6 32.8 %exchange.1 = (f32[6,32768]{1,0:T(8,128)}, f32[5,512,128]{2,1,0:T(8,128)}, f32[8,512]{1,0:T(8,128)}, s32[8,128]{1,0:T(8,128)}, f32[8,256]{1,0:T(8,128)}) custom-call(f32[6,32768]{1,0:T(8,128)} %orbit_in.1, f32[3,32768]{1,0:T(4,128)} %props_in.1, f32[1,64]{1,0:T(1,128)} %bitcast.5, s32[1,256]{1,0:T(1,128)} %bitcast.4), custom_call_target="tpu_custom_call" | custom-call | tf_op jit(solution)/shard_map/exchange/pallas_call | solution.py:422
  33.4 34.9 %pairs.1 = (f32[6,32768]{1,0:T(8,128)}, f32[512,128]{1,0:T(8,128)}) custom-call(f32[6,32768]{1,0:T(8,128)} %get-tuple-element.9.next_in, f32[5,512,128]{2,1,0:T(8,128)} %get-tuple-element.10.grouped, s32[8,128]{1,0:T(8,128)} %get-tuple-element.11.counts), custom_call_target="tpu_custom_call" | custom-call | tf_op jit(solution)/shard_map/pairs/pallas_call | solution.py:462
  68.3 10.8 %bring_home.1 = f32[256,128]{1,0:T(8,128)} custom-call(f32[512,128]{1,0:T(8,128)} %get-tuple-element.13.rate, f32[8,512]{1,0:T(8,128)} %get-tuple-element.14.place, f32[8,256]{1,0:T(8,128)} %get-tuple-element.15.slot), custom_call_target="tpu_custom_call" | custom-call | tf_op jit(solution)/shard_map/bring_home/pallas_call | solution.py:481
  79.1 1.6 %copy.7 = f32[32768]{0:T(1024)} copy(f32[32768]{0:T(1024)} %bitcast.3) | data formatting | bytes 262144

commit v5 on v4

--- a/solution.py
+++ b/solution.py
@@ -338,9 +338,9 @@
     return place, jnp.concatenate(cubes + [jnp.zeros((4, BLK), jnp.int32)], axis=0)
 
 
-def pair_kernel(next_in, grouped, counts, next_out, rate, left, right, sem):
-    next_copy = pltpu.make_async_copy(next_in, next_out, sem)
-    next_copy.start()
+def pair_kernel(next_in, grouped, counts, next_out, rate, left, right, moved, sem):
+    next_load = pltpu.make_async_copy(next_in, moved, sem.at[0])
+    next_load.start()
     lefts, rights = features([grouped[c] for c in range(5)])
     zero = jnp.zeros((SLOTS, BLK), F32)
     for f in range(KF):
@@ -351,6 +351,9 @@
     off_diag = iota((BLK, BLK), 0) != iota((BLK, BLK), 1)
 
     rate[...] = zero
+    next_load.wait()
+    next_copy = pltpu.make_async_copy(moved, next_out, sem.at[1])
+    next_copy.start()
 
     def one_cube(q, members):
         base = q * MOST
@@ -470,7 +473,8 @@
         scratch_shapes=[
             pltpu.VMEM((KF * PITCH, BLK), F32),
             pltpu.VMEM((KF * PITCH, BLK), F32),
-            DMA,
+            pltpu.VMEM(next_state.shape, F32),
+            DMA((2,)),
         ],
         compiler_params=pltpu.CompilerParams(vmem_limit_bytes=LIMIT),
         name="pairs",

time: 80.9 us -> 62.4 us (0.77)
  Pallas kernels: 78.5 us -> 60 us
    pallas_call x1, Pallas kernels: 34.9 us -> 16.6 us  [pair_call(): pl.pallas_call(pair_kernel, out_shape=(jax.ShapeDtypeStruct(next_state.sh...]
where the time goes in v5:
time: 62.4 us; the launch traced here: 62.2 us
  Pallas kernels  60 us (96%)
  local copies, waits for them, and re-layouts  1.57 us (3%)
  between operations  0.65 us (1%)
    pallas_call x1, Pallas kernels, exchange_call(): pl.pallas_call(exchange_kernel, out_shape=(jax.ShapeDtypeStruct((6, many)...  32.8 us
    pallas_call x1, Pallas kernels, pair_call(): pl.pallas_call(pair_kernel, out_shape=(jax.ShapeDtypeStruct(next_state.sh...  16.6 us
    pallas_call x1, Pallas kernels, return_call(): pl.pallas_call(return_kernel, out_shape=jax.ShapeDtypeStruct((NB, BLK), F...  10.6 us
    unnamed x1, local copies, waits for them, and re-layouts  1.57 us

profile of v5, /device:TPU:0, one launch (start us, length us, event | category | flops | bytes accessed | tf_op | source)
XLA Modules:
  0.0 62.2 jit_solution(4664457475038154835)
XLA Ops:
  0.6 32.8 %exchange.1 = (f32[6,32768]{1,0:T(8,128)}, f32[5,512,128]{2,1,0:T(8,128)}, f32[8,512]{1,0:T(8,128)}, s32[8,128]{1,0:T(8,128)}, f32[8,256]{1,0:T(8,128)}) custom-call(f32[6,32768]{1,0:T(8,128)} %orbit_in.1, f32[3,32768]{1,0:T(4,128)} %props_in.1, f32[1,64]{1,0:T(1,128)} %bitcast.5, s32[1,256]{1,0:T(1,128)} %bitcast.4), custom_call_target="tpu_custom_call" | custom-call | tf_op jit(solution)/shard_map/exchange/pallas_call | solution.py:425
  33.4 16.6 %pairs.1 = (f32[6,32768]{1,0:T(8,128)}, f32[512,128]{1,0:T(8,128)}) custom-call(f32[6,32768]{1,0:T(8,128)} %get-tuple-element.9.next_in, f32[5,512,128]{2,1,0:T(8,128)} %get-tuple-element.10.grouped, s32[8,128]{1,0:T(8,128)} %get-tuple-element.11.counts), custom_call_target="tpu_custom_call" | custom-call | tf_op jit(solution)/shard_map/pairs/pallas_call | solution.py:465
  50.0 10.6 %bring_home.1 = f32[256,128]{1,0:T(8,128)} custom-call(f32[512,128]{1,0:T(8,128)} %get-tuple-element.13.rate, f32[8,512]{1,0:T(8,128)} %get-tuple-element.14.place, f32[8,256]{1,0:T(8,128)} %get-tuple-element.15.slot), custom_call_target="tpu_custom_call" | custom-call | tf_op jit(solution)/shard_map/bring_home/pallas_call | solution.py:485
  60.6 1.6 %copy.7 = f32[32768]{0:T(1024)} copy(f32[32768]{0:T(1024)} %bitcast.3) | data formatting | bytes 262144

commit v6 on v5

--- a/solution.py
+++ b/solution.py
@@ -16,7 +16,7 @@
 CUBES = 128
 MOST = 4
 SUB = 16
-GROUP = 8
+GROUP = 16
 KF = 32
 PITCH = SLOTS + 8
 
@@ -95,49 +95,29 @@
 
 def hello(me):
     barrier = pltpu.get_barrier_semaphore()
-
-    def tell(k, carry):
+    for k in range(1, NS):
         pl.semaphore_signal(
-            barrier, inc=1, device_id={"space": lax.rem(me + k, NS)}, device_id_type=MESH
+            barrier, inc=1, device_id={"space": (me + k) & (NS - 1)}, device_id_type=MESH
         )
-        return carry
-
-    lax.fori_loop(1, NS, tell, 0)
     return barrier
 
 
 def send_all(me, out_of, into, send_sem, recv_sem):
-    def start(k, carry):
-        to = lax.rem(me + k, NS)
+    for k in range(1, NS):
+        to = (me + k) & (NS - 1)
         pltpu.make_async_remote_copy(
             src_ref=out_of(to),
             dst_ref=into.at[me],
-            send_sem=send_sem.at[to],
-            recv_sem=recv_sem.at[me],
+            send_sem=send_sem,
+            recv_sem=recv_sem,
             device_id={"space": to},
             device_id_type=MESH,
         ).start()
-        return carry
-
-    lax.fori_loop(1, NS, start, 0)
-
-
-def wait_all(me, out_of, into, send_sem, recv_sem):
-    def arrive(k, carry):
-        other = lax.rem(me + k, NS)
-        copy = pltpu.make_async_remote_copy(
-            src_ref=out_of(other),
-            dst_ref=into.at[other],
-            send_sem=send_sem.at[other],
-            recv_sem=recv_sem.at[other],
-            device_id={"space": other},
-            device_id_type=MESH,
-        )
-        copy.wait_recv()
-        copy.wait_send()
-        return carry
-
-    lax.fori_loop(1, NS, arrive, 0)
+
+
+def wait_all(into, sem):
+    others = into.at[pl.ds(0, NS - 1)]
+    pltpu.make_async_copy(others, others, sem).wait()
 
 
 def one_hot(place, n):
@@ -201,7 +181,7 @@
             [ref[pl.ds(k * 8 + c, 8, stride=8), :] for k in range(0, NB, 8)], axis=0
         )
 
-    wait_all(me, lambda to: need, needs, need_send, need_recv)
+    wait_all(needs, need_recv)
     worst = jnp.max(needs[...], axis=0)
     wide = lambda m: jnp.concatenate([worst[m : m + 1]] * 2, axis=1) <= CAP
     slot, local = slots[0], maps[0][1]
@@ -233,7 +213,7 @@
     slope = pltpu.roll(tab, BLK - 1, 1) - tab
     now = tuple(load(rows, c) for c in range(6))
     drag = load(prows, 2) * (DRAG_SCALE * TIME_STEP)
-    now = lax.fori_loop(0, SUB, lambda s, v: substep(*v, drag, tab, slope), now, unroll=2)
+    now = lax.fori_loop(0, SUB, lambda s, v: substep(*v, drag, tab, slope), now, unroll=4)
     for c in range(6):
         for k in range(0, NB, 8):
             rows[pl.ds(k * 8 + c, 8, stride=8), :] = now[c][k : k + 8]
@@ -252,7 +232,7 @@
     for c in range(3):
         recv_b[c, pl.ds(me, 1)] = send_b[c, pl.ds(me, 1)]
 
-    wait_all(me, lambda to: send_a.at[to], recv_a, a_send, a_recv)
+    wait_all(recv_a, a_recv)
     got = jnp.where(mine, recv_a[:, 2 * CAP, :], 0.0)
     ids = jnp.concatenate(
         [jnp.sum(got[4 * q : 4 * q + 4], axis=0, keepdims=True) for q in range(4)], axis=1
@@ -273,8 +253,12 @@
         regroup(4, recv_a[:, CAP : 2 * CAP, :]),
     ]
     for c in range(3):
-        wait_all(me, lambda to: send_b.at[c, to], recv_b.at[c], b_send.at[c], b_recv.at[c])
+        wait_all(recv_b.at[c], b_recv.at[c])
         copies.append(regroup(c, recv_b[c]))
+    wait_all(needs, need_send)
+    wait_all(recv_a, a_send)
+    for c in range(3):
+        wait_all(recv_b.at[c], b_send.at[c])
     for copy in copies:
         copy.wait()
     next_copy.wait()
@@ -410,8 +394,9 @@
     pl.semaphore_wait(barrier, NS - 1)
     send_all(me, lambda to: back.at[to], home, send_sem, recv_sem)
     pick = one_hot_back(slot[0:1, :])
-    wait_all(me, lambda to: back.at[to], home, send_sem, recv_sem)
+    wait_all(home, recv_sem)
     out[...] = picked(pick, home[...].reshape(SLOTS, BLK))
+    wait_all(home, send_sem)
 
 
 VMEM = pl.BlockSpec(memory_space=pltpu.VMEM)
@@ -447,12 +432,12 @@
             pltpu.VMEM((5, SLOTS, BLK), F32),
             DMA((2,)),
             DMA((5,)),
-            DMA((NS,)),
-            DMA((NS,)),
-            DMA((NS,)),
-            DMA((NS,)),
-            DMA((3, NS)),
-            DMA((3, NS)),
+            DMA,
+            DMA,
+            DMA,
+            DMA,
+            DMA((3,)),
+            DMA((3,)),
         ],
         compiler_params=pltpu.CompilerParams(
             collective_id=0, has_side_effects=True, vmem_limit_bytes=LIMIT
@@ -490,8 +475,8 @@
         scratch_shapes=[
             pltpu.VMEM((NS, CAP, BLK), F32),
             pltpu.VMEM((NS, CAP, BLK), F32),
-            DMA((NS,)),
-            DMA((NS,)),
+            DMA,
+            DMA,
         ],
         compiler_params=pltpu.CompilerParams(
             collective_id=1, has_side_effects=True, vmem_limit_bytes=LIMIT

time: 62.4 us -> 59.7 us (0.957)
  Pallas kernels: 60 us -> 57.2 us
    pallas_call x1, Pallas kernels: 16.6 us -> 13.7 us  [pair_call(): pl.pallas_call(pair_kernel, out_shape=(jax.ShapeDtypeStruct(next_state.sh...]
    pallas_call x1, Pallas kernels: 10.6 us -> 12.7 us  [return_call(): pl.pallas_call(return_kernel, out_shape=jax.ShapeDtypeStruct((NB, BLK), F...]
    pallas_call x1, Pallas kernels: 32.8 us -> 30.9 us  [exchange_call(): pl.pallas_call(exchange_kernel, out_shape=(jax.ShapeDtypeStruct((6, many)...]
where the time goes in v6:
time: 59.7 us; the launch traced here: 59.4 us
  Pallas kernels  57.2 us (96%)
  local copies, waits for them, and re-layouts  1.57 us (3%)
  between operations  0.65 us (1%)
    pallas_call x1, Pallas kernels, exchange_call(): pl.pallas_call(exchange_kernel, out_shape=(jax.ShapeDtypeStruct((6, many)...  30.9 us
    pallas_call x1, Pallas kernels, pair_call(): pl.pallas_call(pair_kernel, out_shape=(jax.ShapeDtypeStruct(next_state.sh...  13.7 us
    pallas_call x1, Pallas kernels, return_call(): pl.pallas_call(return_kernel, out_shape=jax.ShapeDtypeStruct((NB, BLK), F...  12.7 us
    unnamed x1, local copies, waits for them, and re-layouts  1.57 us

profile of v6, /device:TPU:0, one launch (start us, length us, event | category | flops | bytes accessed | tf_op | source)
XLA Modules:
  0.0 59.4 jit_solution(15289208874227039716)
XLA Ops:
  0.6 30.9 %exchange.1 = (f32[6,32768]{1,0:T(8,128)}, f32[5,512,128]{2,1,0:T(8,128)}, f32[8,512]{1,0:T(8,128)}, s32[8,128]{1,0:T(8,128)}, f32[8,256]{1,0:T(8,128)}) custom-call(f32[6,32768]{1,0:T(8,128)} %orbit_in.1, f32[3,32768]{1,0:T(4,128)} %props_in.1, f32[1,64]{1,0:T(1,128)} %bitcast.5, s32[1,256]{1,0:T(1,128)} %bitcast.4), custom_call_target="tpu_custom_call" | custom-call | tf_op jit(solution)/shard_map/exchange/pallas_call | solution.py:410
  31.5 13.7 %pairs.1 = (f32[6,32768]{1,0:T(8,128)}, f32[512,128]{1,0:T(8,128)}) custom-call(f32[6,32768]{1,0:T(8,128)} %get-tuple-element.9.next_in, f32[5,512,128]{2,1,0:T(8,128)} %get-tuple-element.10.grouped, s32[8,128]{1,0:T(8,128)} %get-tuple-element.11.counts), custom_call_target="tpu_custom_call" | custom-call | tf_op jit(solution)/shard_map/pairs/pallas_call | solution.py:450
  45.2 12.7 %bring_home.1 = f32[256,128]{1,0:T(8,128)} custom-call(f32[512,128]{1,0:T(8,128)} %get-tuple-element.13.rate, f32[8,512]{1,0:T(8,128)} %get-tuple-element.14.place, f32[8,256]{1,0:T(8,128)} %get-tuple-element.15.slot), custom_call_target="tpu_custom_call" | custom-call | tf_op jit(solution)/shard_map/bring_home/pallas_call | solution.py:470
  57.9 1.6 %copy.7 = f32[32768]{0:T(1024)} copy(f32[32768]{0:T(1024)} %bitcast.3) | data formatting | bytes 262144

commit v7 on v6

--- a/solution.py
+++ b/solution.py
@@ -1,3 +1,5 @@
+import functools
+
 import jax
 import jax.numpy as jnp
 from jax import lax
@@ -12,10 +14,12 @@
 NB = 256
 NS = 16
 CAP = 32
+SENT = 25
 SLOTS = NS * CAP
 CUBES = 128
 MOST = 4
 SUB = 16
+EARLY = 8
 GROUP = 16
 KF = 32
 PITCH = SLOTS + 8
@@ -56,11 +60,9 @@
     return jnp.concatenate(ranks, axis=1)
 
 
-def cube_maps(cube_row):
-    low, high = cube_row & 15, lax.shift_right_logical(cube_row, 4)
-    spread = [(low + f) & 15 for f in (0, high, 5 * high + lax.shift_right_logical(high, 3))]
-    owner = lax.shift_right_logical(cube_row, 7)
-    return [(owner, cube_row & (CUBES - 1))] + [(to, high) for to in spread]
+def balanced(cube, k):
+    high = lax.shift_right_logical(cube, 4)
+    return ((cube & 15) + lax.shift_right_logical(high * (37 * k + 11), 4)) & 15
 
 
 def substep(x, y, z, vx, vy, vz, drag, tab, slope):
@@ -102,12 +104,12 @@
     return barrier
 
 
-def send_all(me, out_of, into, send_sem, recv_sem):
+def send_all(me, count, out_of, into, send_sem, recv_sem):
     for k in range(1, NS):
         to = (me + k) & (NS - 1)
         pltpu.make_async_remote_copy(
-            src_ref=out_of(to),
-            dst_ref=into.at[me],
+            src_ref=out_of.at[to, pl.ds(0, count)],
+            dst_ref=into.at[me, pl.ds(0, count)],
             send_sem=send_sem,
             recv_sem=recv_sem,
             device_id={"space": to},
@@ -115,8 +117,8 @@
         ).start()
 
 
-def wait_all(into, sem):
-    others = into.at[pl.ds(0, NS - 1)]
+def wait_all(count, into, sem):
+    others = into.at[pl.ds(0, NS - 1), pl.ds(0, count)]
     pltpu.make_async_copy(others, others, sem).wait()
 
 
@@ -142,9 +144,9 @@
 
 
 def exchange_kernel(
-    orbit_in, props_in, table, cube, next_out, grouped_out, place_out, count_out, slot_out,
-    orbit, props, rows, prows, need, needs, send_a, send_b, recv_a, recv_b, grouped,
-    local_sem, group_sem, need_send, need_recv, a_send, a_recv, b_send, b_recv,
+    sent, orbit_in, props_in, table, cube, next_out, grouped_out, place_out, count_out, slot_out, found_out,
+    orbit, props, rows, prows, need, needs, send_r, send_w, send_b, recv_r, recv_w, recv_b, grouped,
+    slot_at, place_at, count_at, local_sem, group_sem, need_send, need_recv, sends, recvs,
 ):
     me = lax.axis_index("space")
     barrier = hello(me)
@@ -153,17 +155,32 @@
     props_copy.start()
     orbit_copy.start()
 
-    maps = cube_maps(cube[...])
-    most = []
-    for to, _ in maps:
-        held = jnp.sum(jnp.where(to == iota((NS, NB), 0), 1.0, 0.0), axis=1, keepdims=True)
-        most.append(jnp.broadcast_to(jnp.max(held, axis=0, keepdims=True), (1, BLK)))
-    need[...] = jnp.concatenate(most + [jnp.zeros((4, BLK), F32)], axis=0)
-    needs[pl.ds(me, 1)] = need[...][None]
-    pl.semaphore_wait(barrier, NS - 1)
-    send_all(me, lambda to: need, needs, need_send, need_recv)
-
-    slots = [to.astype(F32) * CAP + rank_row(to.astype(F32)) for to, _ in maps]
+    if sent < CAP:
+        column = columns_of(cube[...].astype(F32)).astype(jnp.int32)
+        to = balanced(column, iota((NB, BLK), 1))
+        most = jnp.zeros((1, BLK), F32)
+        for device in range(NS):
+            held = jnp.sum(jnp.where(to == device, 1.0, 0.0), axis=0, keepdims=True)
+            most = jnp.maximum(most, held)
+        need[...] = most
+        needs[pl.ds(me, 1)] = need[...][None]
+        pl.semaphore_wait(barrier, NS - 1)
+        for k in range(1, NS):
+            pltpu.make_async_remote_copy(
+                src_ref=need,
+                dst_ref=needs.at[me],
+                send_sem=need_send,
+                recv_sem=need_recv,
+                device_id={"space": (me + k) & (NS - 1)},
+                device_id_type=MESH,
+            ).start()
+        recv_r[:, sent:, :] = jnp.zeros((NS, CAP - sent, BLK), F32)
+        recv_w[:, sent + 1 :, :] = jnp.zeros((NS, CAP - sent - 1, BLK), F32)
+        for c in range(3):
+            recv_b[c, :, sent:, :] = jnp.zeros((NS, CAP - sent, BLK), F32)
+    else:
+        pl.semaphore_wait(barrier, NS - 1)
+
     props_copy.wait()
     orbit_copy.wait()
 
@@ -181,17 +198,33 @@
             [ref[pl.ds(k * 8 + c, 8, stride=8), :] for k in range(0, NB, 8)], axis=0
         )
 
-    wait_all(needs, need_recv)
-    worst = jnp.max(needs[...], axis=0)
-    wide = lambda m: jnp.concatenate([worst[m : m + 1]] * 2, axis=1) <= CAP
-    slot, local = slots[0], maps[0][1]
-    for m in (3, 2, 1):
-        slot = jnp.where(wide(m), slots[m], slot)
-        local = jnp.where(wide(m), maps[m][1], local)
-    slot_out[...] = jnp.broadcast_to(slot, (8, NB))
+    tab = jnp.concatenate([table[...], jnp.zeros((1, 64), F32)], axis=1)
+    tab = pltpu.roll(jnp.broadcast_to(tab, (8, BLK)), 1, 1)
+    slope = pltpu.roll(tab, BLK - 1, 1) - tab
+    now = tuple(load(rows, c) for c in range(6))
+    drag = load(prows, 2) * (DRAG_SCALE * TIME_STEP)
+    advance = lambda s, v: substep(*v, drag, tab, slope)
+    now = lax.fori_loop(0, EARLY, advance, now, unroll=4)
+    if sent < CAP:
+        wait_all(1, needs, need_recv)
+        fits = jnp.max(needs[...], axis=0) <= sent
+        lane = iota((1, BLK), 1).astype(F32)
+        first = jnp.min(jnp.where(fits, lane, float(BLK)), axis=1, keepdims=True)
+        found = first < BLK
+        to = balanced(cube[...], jnp.where(found, first, 0.0).astype(jnp.int32))
+        local = lax.shift_right_logical(cube[...], 4)
+    else:
+        found = None
+        to = lax.shift_right_logical(cube[...], 7)
+        local = cube[...] & (CUBES - 1)
+    slot = to.astype(F32) * CAP + rank_row(to.astype(F32))
+    slot_at[...] = jnp.broadcast_to(slot, (8, NB))
+    slot_copy = pltpu.make_async_copy(slot_at, slot_out, local_sem.at[2])
+    slot_copy.start()
     pick = one_hot(slot, SLOTS)
-    send_a[:, :CAP, :] = picked(pick, load(prows, 0)).reshape(NS, CAP, BLK)
-    send_a[:, CAP : 2 * CAP, :] = picked(pick, load(prows, 1)).reshape(NS, CAP, BLK)
+    send_r[...] = picked(pick, load(prows, 0)).reshape(NS, CAP, BLK)
+    send_all(me, sent, send_r, recv_r, sends.at[3], recvs.at[3])
+    send_w[:, :CAP, :] = picked(pick, load(prows, 1)).reshape(NS, CAP, BLK)
     ids = jnp.dot(
         pick, columns_of((local + 1).astype(F32)).astype(BF16), preferred_element_type=F32
     )
@@ -204,22 +237,18 @@
     id_rows = jnp.where(mine, id_rows, 0.0)
     id_rows = id_rows + pltpu.roll(id_rows, 64, 1)
     id_rows = id_rows + pltpu.roll(id_rows, 32, 1)
-    send_a[:, 2 * CAP :, :] = jnp.broadcast_to(id_rows[:, None, :], (NS, 8, BLK))
-    send_all(me, lambda to: send_a.at[to], recv_a, a_send, a_recv)
-    recv_a[pl.ds(me, 1)] = send_a[pl.ds(me, 1)]
-
-    tab = jnp.concatenate([table[...], jnp.zeros((1, 64), F32)], axis=1)
-    tab = pltpu.roll(jnp.broadcast_to(tab, (8, BLK)), 1, 1)
-    slope = pltpu.roll(tab, BLK - 1, 1) - tab
-    now = tuple(load(rows, c) for c in range(6))
-    drag = load(prows, 2) * (DRAG_SCALE * TIME_STEP)
-    now = lax.fori_loop(0, SUB, lambda s, v: substep(*v, drag, tab, slope), now, unroll=4)
+    send_w[:, sent : sent + 1, :] = id_rows[:, None, :]
+    send_all(me, sent + 1, send_w, recv_w, sends.at[4], recvs.at[4])
+    recv_w[pl.ds(me, 1)] = send_w[pl.ds(me, 1)]
+    recv_r[pl.ds(me, 1)] = send_r[pl.ds(me, 1)]
+
+    now = lax.fori_loop(EARLY, SUB, advance, now, unroll=4)
     for c in range(6):
         for k in range(0, NB, 8):
             rows[pl.ds(k * 8 + c, 8, stride=8), :] = now[c][k : k + 8]
     for c in range(3):
         send_b[c] = picked(pick, load(rows, 3 + c)).reshape(NS, CAP, BLK)
-        send_all(me, lambda to: send_b.at[c, to], recv_b.at[c], b_send.at[c], b_recv.at[c])
+        send_all(me, sent, send_b.at[c], recv_b.at[c], sends.at[c], recvs.at[c])
 
     def collect(b, carry):
         col = pl.ds(pl.multiple_of(b * BLK, BLK), BLK)
@@ -232,14 +261,23 @@
     for c in range(3):
         recv_b[c, pl.ds(me, 1)] = send_b[c, pl.ds(me, 1)]
 
-    wait_all(recv_a, a_recv)
-    got = jnp.where(mine, recv_a[:, 2 * CAP, :], 0.0)
+    wait_all(sent + 1, recv_w, recvs.at[4])
+    got = jnp.where(mine, recv_w[:, sent, :], 0.0)
     ids = jnp.concatenate(
         [jnp.sum(got[4 * q : 4 * q + 4], axis=0, keepdims=True) for q in range(4)], axis=1
     )
     place, counts = cube_order(ids)
-    place_out[...] = jnp.broadcast_to(place, (8, SLOTS))
-    count_out[...] = counts
+    place_at[...] = jnp.broadcast_to(place, (8, SLOTS))
+    place_copy = pltpu.make_async_copy(place_at, place_out, local_sem.at[3])
+    place_copy.start()
+    if found is None:
+        count_at[...] = counts
+        found_out[0, 0] = jnp.int32(1)
+    else:
+        found_out[0, 0] = jnp.where(found, 1, 0)[0, 0]
+        count_at[...] = jnp.where(found, jnp.minimum(counts, CUBES), 0)
+    count_copy = pltpu.make_async_copy(count_at, count_out, local_sem.at[4])
+    count_copy.start()
     pick = one_hot(place, SLOTS)
 
     def regroup(c, plane):
@@ -248,20 +286,22 @@
         copy.start()
         return copy
 
-    copies = [
-        regroup(3, recv_a[:, :CAP, :]),
-        regroup(4, recv_a[:, CAP : 2 * CAP, :]),
-    ]
+    copies = [regroup(4, recv_w[:, :CAP, :])]
+    wait_all(sent, recv_r, recvs.at[3])
+    copies.append(regroup(3, recv_r[...]))
     for c in range(3):
-        wait_all(recv_b.at[c], b_recv.at[c])
+        wait_all(sent, recv_b.at[c], recvs.at[c])
         copies.append(regroup(c, recv_b[c]))
-    wait_all(needs, need_send)
-    wait_all(recv_a, a_send)
+    if sent < CAP:
+        wait_all(1, needs, need_send)
+    wait_all(sent + 1, recv_w, sends.at[4])
+    wait_all(sent, recv_r, sends.at[3])
     for c in range(3):
-        wait_all(recv_b.at[c], b_send.at[c])
+        wait_all(sent, recv_b.at[c], sends.at[c])
     for copy in copies:
         copy.wait()
-    next_copy.wait()
+    for copy in (slot_copy, place_copy, count_copy, next_copy):
+        copy.wait()
 
 
 def features(planes):
@@ -386,61 +426,69 @@
     next_copy.wait()
 
 
-def return_kernel(rate, place, slot, out, back, home, send_sem, recv_sem):
+def return_kernel(sent, rate, place, slot, out, back, home, send_sem, recv_sem):
     me = lax.axis_index("space")
     barrier = hello(me)
     back[...] = picked(one_hot_back(place[0:1, :]), rate[...]).reshape(NS, CAP, BLK)
+    if sent < CAP:
+        home[:, sent:, :] = jnp.zeros((NS, CAP - sent, BLK), F32)
     home[pl.ds(me, 1)] = back[pl.ds(me, 1)]
     pl.semaphore_wait(barrier, NS - 1)
-    send_all(me, lambda to: back.at[to], home, send_sem, recv_sem)
+    send_all(me, sent, back, home, send_sem, recv_sem)
     pick = one_hot_back(slot[0:1, :])
-    wait_all(home, recv_sem)
+    wait_all(sent, home, recv_sem)
     out[...] = picked(pick, home[...].reshape(SLOTS, BLK))
-    wait_all(home, send_sem)
+    wait_all(sent, home, send_sem)
 
 
 VMEM = pl.BlockSpec(memory_space=pltpu.VMEM)
 ANY = pl.BlockSpec(memory_space=pl.ANY)
+SMEM = pl.BlockSpec(memory_space=pltpu.SMEM)
 LIMIT = 56 * 2**20
 DMA = pltpu.SemaphoreType.DMA
 
 
-def exchange_call(orbit_state, object_props, table, cube):
+def exchange_call(sent, orbit_state, object_props, table, cube):
     many = NB * BLK
+    wide = pltpu.VMEM((NS, CAP if sent < CAP else CAP + 8, BLK), F32)
     return pl.pallas_call(
-        exchange_kernel,
+        functools.partial(exchange_kernel, sent),
         out_shape=(
             jax.ShapeDtypeStruct((6, many), F32),
             jax.ShapeDtypeStruct((5, SLOTS, BLK), F32),
             jax.ShapeDtypeStruct((8, SLOTS), F32),
             jax.ShapeDtypeStruct((8, BLK), jnp.int32),
             jax.ShapeDtypeStruct((8, NB), F32),
+            jax.ShapeDtypeStruct((1, 1), jnp.int32),
         ),
         in_specs=[ANY, ANY, VMEM, VMEM],
-        out_specs=(ANY, ANY, VMEM, VMEM, VMEM),
+        out_specs=(ANY, ANY, ANY, ANY, ANY, SMEM),
         scratch_shapes=[
             pltpu.VMEM((6, many), F32),
             pltpu.VMEM((3, many), F32),
             pltpu.VMEM((NB * 8, BLK), F32),
             pltpu.VMEM((NB * 8, BLK), F32),
-            pltpu.VMEM((8, BLK), F32),
-            pltpu.VMEM((NS, 8, BLK), F32),
-            pltpu.VMEM((NS, 2 * CAP + 8, BLK), F32),
+            pltpu.VMEM((1, BLK), F32),
+            pltpu.VMEM((NS, 1, BLK), F32),
+            pltpu.VMEM((NS, CAP, BLK), F32),
+            wide,
             pltpu.VMEM((3, NS, CAP, BLK), F32),
-            pltpu.VMEM((NS, 2 * CAP + 8, BLK), F32),
+            pltpu.VMEM((NS, CAP, BLK), F32),
+            wide,
             pltpu.VMEM((3, NS, CAP, BLK), F32),
             pltpu.VMEM((5, SLOTS, BLK), F32),
-            DMA((2,)),
+            pltpu.VMEM((8, NB), F32),
+            pltpu.VMEM((8, SLOTS), F32),
+            pltpu.VMEM((8, BLK), jnp.int32),
+            DMA((5,)),
             DMA((5,)),
             DMA,
             DMA,
-            DMA,
-            DMA,
-            DMA((3,)),
-            DMA((3,)),
+            DMA((5,)),
+            DMA((5,)),
         ],
         compiler_params=pltpu.CompilerParams(
-            collective_id=0, has_side_effects=True, vmem_limit_bytes=LIMIT
+            collective_id=0 if sent < CAP else 2, has_side_effects=True, vmem_limit_bytes=LIMIT
         ),
         name="exchange",
     )(orbit_state, object_props, table, cube)
@@ -453,7 +501,7 @@
             jax.ShapeDtypeStruct(next_state.shape, F32),
             jax.ShapeDtypeStruct((SLOTS, BLK), F32),
         ),
-        in_specs=[ANY, VMEM, pl.BlockSpec(memory_space=pltpu.SMEM)],
+        in_specs=[ANY, VMEM, SMEM],
         out_specs=(ANY, VMEM),
         scratch_shapes=[
             pltpu.VMEM((KF * PITCH, BLK), F32),
@@ -466,9 +514,9 @@
     )(next_state, grouped, counts)
 
 
-def return_call(rate, place, slot):
+def return_call(sent, rate, place, slot):
     return pl.pallas_call(
-        return_kernel,
+        functools.partial(return_kernel, sent),
         out_shape=jax.ShapeDtypeStruct((NB, BLK), F32),
         in_specs=[VMEM, VMEM, VMEM],
         out_specs=VMEM,
@@ -479,18 +527,26 @@
             DMA,
         ],
         compiler_params=pltpu.CompilerParams(
-            collective_id=1, has_side_effects=True, vmem_limit_bytes=LIMIT
+            collective_id=1 if sent < CAP else 3, has_side_effects=True, vmem_limit_bytes=LIMIT
         ),
         name="bring_home",
     )(rate, place, slot)
 
 
 def on_device(orbit_state, object_props, density_table, block_cube):
-    moved, grouped, place, counts, slot = exchange_call(
-        orbit_state, object_props, density_table.reshape(1, 64), block_cube.reshape(1, NB)
-    )
-    next_state, rate = pair_call(moved, grouped, counts)
-    return next_state, return_call(rate, place, slot).reshape(NB * BLK)
+    args = (orbit_state, object_props, density_table.reshape(1, 64), block_cube.reshape(1, NB))
+
+    def attempt(sent):
+        moved, grouped, place, counts, slot, found = exchange_call(sent, *args)
+        next_state, rate = pair_call(moved, grouped, counts)
+        return next_state, return_call(sent, rate, place, slot), found.reshape(())
+
+    def again(carry):
+        return (attempt(CAP)[1], jnp.int32(1))
+
+    next_state, rate, found = attempt(SENT)
+    rate, _ = lax.while_loop(lambda carry: carry[1] == 0, again, (rate, found))
+    return next_state, rate.reshape(NB * BLK)
 
 
 def solution(mesh):

time: 59.7 us -> 56.9 us (0.953)
  Pallas kernels: 57.2 us -> 53.8 us
  loops' own time: 0 us -> 0.64 us
    pallas_call x2, Pallas kernels: 43.5 us -> 38.7 us  [the longest x1 26.5 us: exchange_call(): pl.pallas_call(functools.partial(exchange_kernel, sent), out_shape=(jax.S...]
    pallas_call x1, Pallas kernels: 13.7 us -> 15.1 us  [pair_call(): pl.pallas_call(pair_kernel, out_shape=(jax.ShapeDtypeStruct(next_state.sh...]
    another operation x0 -> x1, loops' own time: none -> 0.64 us  [on_device(): rate, _ = lax.while_loop(lambda carry: carry[1] == 0, again, (rate, found))]
    unnamed x1 -> x9, local copies, waits for them, and re-layouts: 1.57 us -> 1.59 us
where the time goes in v7:
time: 56.9 us; the launch traced here: 56.7 us
  Pallas kernels  53.8 us (95%)
  local copies, waits for them, and re-layouts  1.59 us (3%)
  between operations  0.72 us (1%)
  loops' own time  0.64 us (1%)
    pallas_call x1, Pallas kernels, exchange_call(): pl.pallas_call(functools.partial(exchange_kernel, sent), out_shape=(jax.S...  26.5 us
    pallas_call x1, Pallas kernels, pair_call(): pl.pallas_call(pair_kernel, out_shape=(jax.ShapeDtypeStruct(next_state.sh...  15.1 us
    pallas_call x1, Pallas kernels, return_call(): pl.pallas_call(functools.partial(return_kernel, sent), out_shape=jax.Shap...  12.1 us
    unnamed x9, local copies, waits for them, and re-layouts  1.59 us

profile of v7, /device:TPU:0, one launch (start us, length us, event | category | flops | bytes accessed | tf_op | source)
XLA Modules:
  0.0 56.7 jit_solution(8658716069056618095)
XLA Ops:
  0.6 26.5 %exchange.3 = (f32[6,32768]{1,0:T(8,128)}, f32[5,512,128]{2,1,0:T(8,128)}, f32[8,512]{1,0:T(8,128)}, s32[8,128]{1,0:T(8,128)}, f32[8,256]{1,0:T(8,128)}, /*index=5*/s32[1,1]{1,0:T(1,128)}) custom-call(f32[6,32768]{1,0:T(8,128)} %orbit_in.1, f32[3,32768]{1,0:T(4,128)} %props_in.1, f32[1,64]{1,0:T(1,128)} %bitcast.7, s32[1,256]{1,0:T(1,128)} %bitcast.5), custom_call_target="tpu_custom_call" | custom-call | tf_op jit(solution)/shard_map/exchange/pallas_call | solution.py:454
  27.2 0.0 copy-start
  27.2 0.0 copy-start.1
  27.2 0.0 copy-start.2
  27.2 0.0 copy-start.3
  27.2 15.1 %pairs.3 = (f32[6,32768]{1,0:T(8,128)}, f32[512,128]{1,0:T(8,128)}) custom-call(f32[6,32768]{1,0:T(8,128)} %get-tuple-element.46.next_in, f32[5,512,128]{2,1,0:T(8,128)} %get-tuple-element.47.grouped, s32[8,128]{1,0:T(8,128)} %get-tuple-element.48.counts), custom_call_target="tpu_custom_call" | custom-call | tf_op jit(solution)/shard_map/pairs/pallas_call | solution.py:498
  42.3 12.1 %bring_home.3 = f32[256,128]{1,0:T(8,128)} custom-call(f32[512,128]{1,0:T(8,128)} %get-tuple-element.50.rate, f32[8,512]{1,0:T(8,128)} %get-tuple-element.51.place, f32[8,256]{1,0:T(8,128)} %get-tuple-element.52.slot), custom_call_target="tpu_custom_call" | custom-call | tf_op jit(solution)/shard_map/bring_home/pallas_call | solution.py:518
  54.5 0.0 copy-done
  54.5 0.0 copy-done.1
  54.5 0.0 copy-done.2
  54.5 0.0 copy-done.3
  54.5 0.6 %while.9 = (f32[256,128]{1,0:T(8,128)}, s32[]{:T(128)}, f32[6,32768]{1,0:T(8,128)S(1)}, f32[3,32768]{1,0:T(4,128)S(1)}, f32[1,64]{1,0:T(1,128)S(1)}, /*index=5*/s32[1,256]{1,0:T(1,128)S(1)}) while((f32[256,128]{1,0:T(8,128)}, s32[]{:T(128)}, f32[6,32768]{1,0:T(8,128)S(1)}, f32[3,32768]{1,0:T(4,128)S(1)}, f32[1,64]{1,0:T(1,128)S(1)}, ...), condition=%region_1.0_spmd, body=%region_0.0_spmd | while | flops 1 | bytes 65 | solution.py:548
  55.1 1.6 %copy.15 = f32[32768]{0:T(1024)} copy(f32[32768]{0:T(1024)} %bitcast.4) | data formatting | bytes 262144
Async XLA Ops:
  27.2 27.3 %copy-start = (f32[6,32768]{1,0:T(8,128)S(1)}, f32[6,32768]{1,0:T(8,128)}, u32[]{:S(2)}) copy-start(f32[6,32768]{1,0:T(8,128)} %orbit_in.1) | copy-start | bytes 2359300
  27.2 27.3 %copy-start.1 = (f32[3,32768]{1,0:T(4,128)S(1)}, f32[3,32768]{1,0:T(4,128)}, u32[]{:S(2)}) copy-start(f32[3,32768]{1,0:T(4,128)} %props_in.1) | copy-start | bytes 1179652
  27.2 27.3 %copy-start.2 = (s32[256]{0:T(256)S(1)}, s32[256]{0:T(256)}, u32[]{:S(2)}) copy-start(s32[256]{0:T(256)} %param.9) | copy-start | bytes 3076
  27.2 27.3 %copy-start.3 = (f32[64]{0:T(128)S(1)}, f32[64]{0:T(128)}, u32[]{:S(2)}) copy-start(f32[64]{0:T(128)} %param.8) | copy-start | bytes 772

commit v8 on v7

--- a/solution.py
+++ b/solution.py
@@ -18,6 +18,7 @@
 SLOTS = NS * CAP
 CUBES = 128
 MOST = 4
+NTAB = 64
 SUB = 16
 EARLY = 8
 GROUP = 16
@@ -144,16 +145,21 @@
 
 
 def exchange_kernel(
-    sent, orbit_in, props_in, table, cube, next_out, grouped_out, place_out, count_out, slot_out, found_out,
+    sent, orbit_in, props_in, table_in, cube_in, next_out, grouped_out, place_out, count_out, slot_out, found_out,
     orbit, props, rows, prows, need, needs, send_r, send_w, send_b, recv_r, recv_w, recv_b, grouped,
-    slot_at, place_at, count_at, local_sem, group_sem, need_send, need_recv, sends, recvs,
+    slot_at, place_at, count_at, table, cube, local_sem, group_sem, need_send, need_recv, sends, recvs,
 ):
     me = lax.axis_index("space")
+    cube_copy = pltpu.make_async_copy(cube_in, cube, local_sem.at[5])
+    table_copy = pltpu.make_async_copy(table_in, table, local_sem.at[6])
+    cube_copy.start()
     barrier = hello(me)
+    table_copy.start()
     orbit_copy = pltpu.make_async_copy(orbit_in, orbit, local_sem.at[0])
     props_copy = pltpu.make_async_copy(props_in, props, local_sem.at[1])
     props_copy.start()
     orbit_copy.start()
+    cube_copy.wait()
 
     if sent < CAP:
         column = columns_of(cube[...].astype(F32)).astype(jnp.int32)
@@ -181,6 +187,7 @@
     else:
         pl.semaphore_wait(barrier, NS - 1)
 
+    table_copy.wait()
     props_copy.wait()
     orbit_copy.wait()
 
@@ -426,9 +433,20 @@
     next_copy.wait()
 
 
-def return_kernel(sent, rate, place, slot, out, back, home, send_sem, recv_sem):
+def return_kernel(
+    sent, rate_in, place_in, slot_in, out, rate, place, slot, back, home, local_sem, send_sem, recv_sem
+):
     me = lax.axis_index("space")
+    place_copy = pltpu.make_async_copy(place_in, place, local_sem.at[0])
+    rate_copy = pltpu.make_async_copy(rate_in, rate, local_sem.at[1])
+    slot_copy = pltpu.make_async_copy(slot_in, slot, local_sem.at[2])
+    place_copy.start()
+    rate_copy.start()
+    slot_copy.start()
     barrier = hello(me)
+    place_copy.wait()
+    rate_copy.wait()
+    slot_copy.wait()
     back[...] = picked(one_hot_back(place[0:1, :]), rate[...]).reshape(NS, CAP, BLK)
     if sent < CAP:
         home[:, sent:, :] = jnp.zeros((NS, CAP - sent, BLK), F32)
@@ -461,7 +479,7 @@
             jax.ShapeDtypeStruct((8, NB), F32),
             jax.ShapeDtypeStruct((1, 1), jnp.int32),
         ),
-        in_specs=[ANY, ANY, VMEM, VMEM],
+        in_specs=[ANY, ANY, ANY, ANY],
         out_specs=(ANY, ANY, ANY, ANY, ANY, SMEM),
         scratch_shapes=[
             pltpu.VMEM((6, many), F32),
@@ -480,7 +498,9 @@
             pltpu.VMEM((8, NB), F32),
             pltpu.VMEM((8, SLOTS), F32),
             pltpu.VMEM((8, BLK), jnp.int32),
-            DMA((5,)),
+            pltpu.VMEM((1, NTAB), F32),
+            pltpu.VMEM((1, NB), jnp.int32),
+            DMA((7,)),
             DMA((5,)),
             DMA,
             DMA,
@@ -518,11 +538,15 @@
     return pl.pallas_call(
         functools.partial(return_kernel, sent),
         out_shape=jax.ShapeDtypeStruct((NB, BLK), F32),
-        in_specs=[VMEM, VMEM, VMEM],
+        in_specs=[ANY, ANY, ANY],
         out_specs=VMEM,
         scratch_shapes=[
+            pltpu.VMEM((SLOTS, BLK), F32),
+            pltpu.VMEM((8, SLOTS), F32),
+            pltpu.VMEM((8, NB), F32),
             pltpu.VMEM((NS, CAP, BLK), F32),
             pltpu.VMEM((NS, CAP, BLK), F32),
+            DMA((3,)),
             DMA,
             DMA,
         ],

time: 56.9 us -> 53.6 us (0.942)
  Pallas kernels: 53.8 us -> 50.5 us
    pallas_call x1, Pallas kernels: 12.1 us -> 9.48 us  [return_call(): pl.pallas_call(functools.partial(return_kernel, sent), out_shape=jax.Shap...]
    pallas_call x1, Pallas kernels: 26.5 us -> 25.9 us  [exchange_call(): pl.pallas_call(functools.partial(exchange_kernel, sent), out_shape=(jax.S...]
where the time goes in v8:
time: 53.6 us; the launch traced here: 53.4 us
  Pallas kernels  50.5 us (94%)
  local copies, waits for them, and re-layouts  1.59 us (3%)
  between operations  0.72 us (1%)
  loops' own time  0.64 us (1%)
    pallas_call x1, Pallas kernels, exchange_call(): pl.pallas_call(functools.partial(exchange_kernel, sent), out_shape=(jax.S...  25.9 us
    pallas_call x1, Pallas kernels, pair_call(): pl.pallas_call(pair_kernel, out_shape=(jax.ShapeDtypeStruct(next_state.sh...  15.1 us
    pallas_call x1, Pallas kernels, return_call(): pl.pallas_call(functools.partial(return_kernel, sent), out_shape=jax.Shap...  9.48 us
    unnamed x9, local copies, waits for them, and re-layouts  1.59 us

profile of v8, /device:TPU:0, one launch (start us, length us, event | category | flops | bytes accessed | tf_op | source)
XLA Modules:
  0.0 53.4 jit_solution(15453769429286850795)
XLA Ops:
  0.6 25.9 %exchange.3 = (f32[6,32768]{1,0:T(8,128)}, f32[5,512,128]{2,1,0:T(8,128)}, f32[8,512]{1,0:T(8,128)}, s32[8,128]{1,0:T(8,128)}, f32[8,256]{1,0:T(8,128)}, /*index=5*/s32[1,1]{1,0:T(1,128)}) custom-call(f32[6,32768]{1,0:T(8,128)} %orbit_in.1, f32[3,32768]{1,0:T(4,128)} %props_in.1, f32[1,64]{1,0:T(1,128)} %bitcast.7, s32[1,256]{1,0:T(1,128)} %bitcast.5), custom_call_target="tpu_custom_call" | custom-call | tf_op jit(solution)/shard_map/exchange/pallas_call | solution.py:472
  26.5 0.0 copy-start
  26.5 0.0 copy-start.1
  26.6 0.0 copy-start.2
  26.6 0.0 copy-start.3
  26.6 15.1 %pairs.3 = (f32[6,32768]{1,0:T(8,128)}, f32[512,128]{1,0:T(8,128)}) custom-call(f32[6,32768]{1,0:T(8,128)} %get-tuple-element.46.next_in, f32[5,512,128]{2,1,0:T(8,128)} %get-tuple-element.47.grouped, s32[8,128]{1,0:T(8,128)} %get-tuple-element.48.counts), custom_call_target="tpu_custom_call" | custom-call | tf_op jit(solution)/shard_map/pairs/pallas_call | solution.py:518
  41.7 9.5 %bring_home.3 = f32[256,128]{1,0:T(8,128)} custom-call(f32[512,128]{1,0:T(8,128)} %get-tuple-element.50.rate_in, f32[8,512]{1,0:T(8,128)} %get-tuple-element.51.place_in, f32[8,256]{1,0:T(8,128)} %get-tuple-element.52.slot_in), custom_call_target="tpu_custom_call" | custom-call | tf_op jit(solution)/shard_map/bring_home/pallas_call | solution.py:538
  51.2 0.0 copy-done
  51.2 0.0 copy-done.1
  51.2 0.0 copy-done.2
  51.2 0.0 copy-done.3
  51.2 0.6 %while.9 = (f32[256,128]{1,0:T(8,128)}, s32[]{:T(128)}, f32[6,32768]{1,0:T(8,128)S(1)}, f32[3,32768]{1,0:T(4,128)S(1)}, f32[1,64]{1,0:T(1,128)S(1)}, /*index=5*/s32[1,256]{1,0:T(1,128)S(1)}) while((f32[256,128]{1,0:T(8,128)}, s32[]{:T(128)}, f32[6,32768]{1,0:T(8,128)S(1)}, f32[3,32768]{1,0:T(4,128)S(1)}, f32[1,64]{1,0:T(1,128)S(1)}, ...), condition=%region_1.0_spmd, body=%region_0.0_spmd | while | flops 1 | bytes 65 | solution.py:572
  51.9 1.6 %copy.15 = f32[32768]{0:T(1024)} copy(f32[32768]{0:T(1024)} %bitcast.4) | data formatting | bytes 262144
Async XLA Ops:
  26.5 24.6 %copy-start = (f32[6,32768]{1,0:T(8,128)S(1)}, f32[6,32768]{1,0:T(8,128)}, u32[]{:S(2)}) copy-start(f32[6,32768]{1,0:T(8,128)} %orbit_in.1) | copy-start | bytes 2359300
  26.5 24.6 %copy-start.1 = (f32[3,32768]{1,0:T(4,128)S(1)}, f32[3,32768]{1,0:T(4,128)}, u32[]{:S(2)}) copy-start(f32[3,32768]{1,0:T(4,128)} %props_in.1) | copy-start | bytes 1179652
  26.6 24.6 %copy-start.2 = (s32[256]{0:T(256)S(1)}, s32[256]{0:T(256)}, u32[]{:S(2)}) copy-start(s32[256]{0:T(256)} %param.9) | copy-start | bytes 3076
  26.6 24.6 %copy-start.3 = (f32[64]{0:T(128)S(1)}, f32[64]{0:T(128)}, u32[]{:S(2)}) copy-start(f32[64]{0:T(128)} %param.8) | copy-start | bytes 772

commit v9 on v8

--- a/solution.py
+++ b/solution.py
@@ -21,9 +21,10 @@
 NTAB = 64
 SUB = 16
 EARLY = 8
-GROUP = 16
+GROUPS = (8, 16, 16, 32)
+SPARE = MOST * 32
 KF = 32
-PITCH = SLOTS + 8
+PITCH = SLOTS + SPARE + 8
 
 TIME_STEP = 0.2
 EARTH_SPIN = 0.0588
@@ -381,7 +382,7 @@
     gap_rows = iota((KF, BLK), 0) < 18
     off_diag = iota((BLK, BLK), 0) != iota((BLK, BLK), 1)
 
-    rate[...] = zero
+    rate[:SLOTS, :] = zero
     next_load.wait()
     next_copy = pltpu.make_async_copy(moved, next_out, sem.at[1])
     next_copy.start()
@@ -419,16 +420,16 @@
             rate[pl.ds(base + c, 1), :] = jnp.sum(total, axis=0, keepdims=True) * (1.0 / (MOST * BLK))
 
     done = 0
-    for row, members in enumerate(range(MOST, 0, -1)):
-        upto = lax.div(counts[row, 0] + (GROUP - 1), GROUP)
-
-        def group(g, carry, members=members):
-            for k in range(GROUP):
-                one_cube(g * GROUP + k, members)
+    for row, size in enumerate(GROUPS):
+        steps = lax.div(jnp.maximum(counts[row, 0] - done, 0) + (size - 1), size)
+
+        def group(g, carry, first=done, size=size, members=MOST - row):
+            for k in range(size):
+                one_cube(first + g * size + k, members)
             return carry
 
-        lax.fori_loop(done, upto, group, 0)
-        done = upto
+        lax.fori_loop(0, steps, group, 0)
+        done = done + steps * size
 
     next_copy.wait()
 
@@ -447,7 +448,7 @@
     place_copy.wait()
     rate_copy.wait()
     slot_copy.wait()
-    back[...] = picked(one_hot_back(place[0:1, :]), rate[...]).reshape(NS, CAP, BLK)
+    back[...] = picked(one_hot_back(place[0:1, :]), rate[:SLOTS, :]).reshape(NS, CAP, BLK)
     if sent < CAP:
         home[:, sent:, :] = jnp.zeros((NS, CAP - sent, BLK), F32)
     home[pl.ds(me, 1)] = back[pl.ds(me, 1)]
@@ -519,7 +520,7 @@
         pair_kernel,
         out_shape=(
             jax.ShapeDtypeStruct(next_state.shape, F32),
-            jax.ShapeDtypeStruct((SLOTS, BLK), F32),
+            jax.ShapeDtypeStruct((SLOTS + SPARE, BLK), F32),
         ),
         in_specs=[ANY, VMEM, SMEM],
         out_specs=(ANY, VMEM),
@@ -541,7 +542,7 @@
         in_specs=[ANY, ANY, ANY],
         out_specs=VMEM,
         scratch_shapes=[
-            pltpu.VMEM((SLOTS, BLK), F32),
+            pltpu.VMEM((SLOTS + SPARE, BLK), F32),
             pltpu.VMEM((8, SLOTS), F32),
             pltpu.VMEM((8, NB), F32),
             pltpu.VMEM((NS, CAP, BLK), F32),

time: 53.6 us -> 54.6 us (1.019)
  Pallas kernels: 50.5 us -> 52 us
    pallas_call x1, Pallas kernels: 15.1 us -> 16.8 us  [pair_call(): pl.pallas_call(pair_kernel, out_shape=(jax.ShapeDtypeStruct(next_state.sh...]
where the time goes in v9:
time: 54.6 us; the launch traced here: 54.9 us
  Pallas kernels  52 us (95%)
  local copies, waits for them, and re-layouts  1.59 us (3%)
  between operations  0.72 us (1%)
  loops' own time  0.63 us (1%)
    pallas_call x1, Pallas kernels, exchange_call(): pl.pallas_call(functools.partial(exchange_kernel, sent), out_shape=(jax.S...  25.9 us
    pallas_call x1, Pallas kernels, pair_call(): pl.pallas_call(pair_kernel, out_shape=(jax.ShapeDtypeStruct(next_state.sh...  16.8 us
    pallas_call x1, Pallas kernels, return_call(): pl.pallas_call(functools.partial(return_kernel, sent), out_shape=jax.Shap...  9.3 us
    unnamed x9, local copies, waits for them, and re-layouts  1.59 us

profile of v9, /device:TPU:0, one launch (start us, length us, event | category | flops | bytes accessed | tf_op | source)
XLA Modules:
  0.0 54.9 jit_solution(7776650888553847343)
XLA Ops:
  0.6 25.9 %exchange.3 = (f32[6,32768]{1,0:T(8,128)}, f32[5,512,128]{2,1,0:T(8,128)}, f32[8,512]{1,0:T(8,128)}, s32[8,128]{1,0:T(8,128)}, f32[8,256]{1,0:T(8,128)}, /*index=5*/s32[1,1]{1,0:T(1,128)}) custom-call(f32[6,32768]{1,0:T(8,128)} %orbit_in.1, f32[3,32768]{1,0:T(4,128)} %props_in.1, f32[1,64]{1,0:T(1,128)} %bitcast.7, s32[1,256]{1,0:T(1,128)} %bitcast.5), custom_call_target="tpu_custom_call" | custom-call | tf_op jit(solution)/shard_map/exchange/pallas_call | solution.py:473
  26.5 0.0 copy-start
  26.5 0.0 copy-start.1
  26.6 0.0 copy-start.2
  26.6 0.0 copy-start.3
  26.6 16.8 %pairs.3 = (f32[6,32768]{1,0:T(8,128)}, f32[640,128]{1,0:T(8,128)}) custom-call(f32[6,32768]{1,0:T(8,128)} %get-tuple-element.46.next_in, f32[5,512,128]{2,1,0:T(8,128)} %get-tuple-element.47.grouped, s32[8,128]{1,0:T(8,128)} %get-tuple-element.48.counts), custom_call_target="tpu_custom_call" | custom-call | tf_op jit(solution)/shard_map/pairs/pallas_call | solution.py:519
  43.4 9.3 %bring_home.3 = f32[256,128]{1,0:T(8,128)} custom-call(f32[640,128]{1,0:T(8,128)} %get-tuple-element.50.rate_in, f32[8,512]{1,0:T(8,128)} %get-tuple-element.51.place_in, f32[8,256]{1,0:T(8,128)} %get-tuple-element.52.slot_in), custom_call_target="tpu_custom_call" | custom-call | tf_op jit(solution)/shard_map/bring_home/pallas_call | solution.py:539
  52.7 0.0 copy-done
  52.7 0.0 copy-done.1
  52.7 0.0 copy-done.2
  52.7 0.0 copy-done.3
  52.7 0.6 %while.9 = (f32[256,128]{1,0:T(8,128)}, s32[]{:T(128)}, f32[6,32768]{1,0:T(8,128)S(1)}, f32[3,32768]{1,0:T(4,128)S(1)}, f32[1,64]{1,0:T(1,128)S(1)}, /*index=5*/s32[1,256]{1,0:T(1,128)S(1)}) while((f32[256,128]{1,0:T(8,128)}, s32[]{:T(128)}, f32[6,32768]{1,0:T(8,128)S(1)}, f32[3,32768]{1,0:T(4,128)S(1)}, f32[1,64]{1,0:T(1,128)S(1)}, ...), condition=%region_1.0_spmd, body=%region_0.0_spmd | while | flops 1 | bytes 65 | solution.py:573
  53.4 1.6 %copy.15 = f32[32768]{0:T(1024)} copy(f32[32768]{0:T(1024)} %bitcast.4) | data formatting | bytes 262144
Async XLA Ops:
  26.5 26.2 %copy-start = (f32[6,32768]{1,0:T(8,128)S(1)}, f32[6,32768]{1,0:T(8,128)}, u32[]{:S(2)}) copy-start(f32[6,32768]{1,0:T(8,128)} %orbit_in.1) | copy-start | bytes 2359300
  26.5 26.2 %copy-start.1 = (f32[3,32768]{1,0:T(4,128)S(1)}, f32[3,32768]{1,0:T(4,128)}, u32[]{:S(2)}) copy-start(f32[3,32768]{1,0:T(4,128)} %props_in.1) | copy-start | bytes 1179652
  26.6 26.2 %copy-start.2 = (s32[256]{0:T(256)S(1)}, s32[256]{0:T(256)}, u32[]{:S(2)}) copy-start(s32[256]{0:T(256)} %param.9) | copy-start | bytes 3076
  26.6 26.2 %copy-start.3 = (f32[64]{0:T(128)S(1)}, f32[64]{0:T(128)}, u32[]{:S(2)}) copy-start(f32[64]{0:T(128)} %param.8) | copy-start | bytes 772
